TPU v7x, 512 devices: a whole 4x8x8 slice. The times are simulated.
512 devices in a mesh: dp: 32 (over y, x), seq: 16 (over z, core).
Axes of the slice: x: 4, y: 8, z: 8, core: 2. Of those that a mesh axis runs over, the one named last changes fastest.
Arguments:
- queries: bfloat16 [32, 2048, 512], P('dp', 'seq'), may hold values from -6 to 6
- keys: bfloat16 [32, 2048, 512], P('dp', 'seq'), may hold values from -6 to 6
- values: bfloat16 [32, 2048, 512], P('dp', 'seq'), may hold values from -6 to 6
- grad_out: bfloat16 [32, 2048, 512], P('dp', 'seq'), may hold values from -6 to 6
- random_blocks: int32 [32, 32, 3], P('dp', 'seq'), may hold values from 0 to 31, as said below
- proj: bfloat16 [512, 512], P('dp'), may hold values from -0.25 to 0.25
Outputs:
- grad_queries: bfloat16 [32, 2048, 512], P('dp', 'seq')
- grad_keys: bfloat16 [32, 2048, 512], P('dp', 'seq')
- grad_values: bfloat16 [32, 2048, 512], P('dp', 'seq')
- grad_proj: float32 [512, 512], P('dp')
Inputs may be any that keep to these rules, and one draw needn't show every extreme that they name: `random_blocks`: A query block's random blocks lie outside the 2 blocks of its own index of seq; of the 6 random blocks of one index of seq, at most 1 lie on the blocks of any one other index, and exactly 1 on some.
All inputs are finite; a program needn't handle non-finite values.
Results may differ from a plain program's by a relative error of at most 0.029.
Values may be sent and summed in bfloat16 or wider, within the bound.
A program may use at most 64 MiB of HBM per device.

v0:
```python
import jax
import jax.numpy as jnp
from jax import lax
from jax.sharding import PartitionSpec as P

HEADS = 8
HEAD_DIM = 64
BLOCK = 64
RANDOM = 3


def extended(cells, sides, width):
    for axis, dim in sides:
        count = lax.axis_size(axis)
        ends = count - 1
        head = lax.slice_in_dim(cells, 0, width, axis=dim)
        tail = lax.slice_in_dim(cells, cells.shape[dim] - width, cells.shape[dim], axis=dim)
        cells = jnp.concatenate(
            [
                lax.ppermute(tail, axis, [(i, (i + 1) % count) for i in range(ends)]),
                cells,
                lax.ppermute(head, axis, [((i + 1) % count, i) for i in range(ends)]),
            ],
            axis=dim,
        )
    return cells


def spread(value, axis, source):
    kept = jnp.where(lax.axis_index(axis) == source, value, 0).astype(value.dtype)
    return lax.psum(kept, axis)


def slot_table(rows, random_ids, total):
    rows = rows[:, None]
    fixed = jnp.concatenate(
        [rows - 1, rows, rows + 1, jnp.zeros_like(rows), jnp.ones_like(rows)], axis=1
    )
    block_ids = jnp.concatenate([fixed, random_ids], axis=1)
    width_slots = block_ids.shape[1]
    inside = (block_ids >= 0) & (block_ids < total)
    order = jnp.arange(width_slots, dtype=jnp.int32)
    before = order[None, :] < order[:, None]
    clash = (
        (block_ids[:, :, None] == block_ids[:, None, :]) & inside[:, None, :] & before[None, :, :]
    )
    valid = inside & jnp.logical_not(jnp.any(clash, axis=2))
    return (block_ids, valid)


def per_device(queries, keys, values, grad_out, random_blocks, proj):
    tokens = queries.shape[1]
    width = queries.shape[2]
    local = tokens // BLOCK
    count = 5 + RANDOM
    scale = HEAD_DIM ** (-0.5)
    seq_count = lax.axis_size("seq")
    seq_index = lax.axis_index("seq")
    total = local * seq_count
    capacity = (local * RANDOM + seq_count - 2) // (seq_count - 1)
    requests = local * RANDOM
    flat_slots = seq_count * capacity
    lists = lax.all_gather(random_blocks, "seq", axis=1, tiled=True)[0]
    asked = lists.reshape(seq_count, requests)
    owner = asked // local
    within = asked % local
    peers = jnp.arange(seq_count, dtype=jnp.int32)
    same_owner = owner[:, :, None] == peers[None, None, :]
    ranks = jnp.cumsum(same_owner.astype(jnp.int32), axis=1) - 1
    slot_of = jnp.sum(jnp.where(same_owner, ranks, 0), axis=2)
    positions_all = owner * capacity + slot_of
    my_positions = lax.dynamic_index_in_dim(positions_all, seq_index, 0, keepdims=False)
    to_me = owner == seq_index
    slot_hit = to_me[:, :, None] & (
        slot_of[:, :, None] == jnp.arange(capacity, dtype=jnp.int32)[None, None, :]
    )
    block_hit = within[:, :, None] == jnp.arange(local, dtype=jnp.int32)[None, None, :]
    table = jnp.einsum(
        "rjc,rju->rcu", slot_hit.astype(jnp.float32), block_hit.astype(jnp.float32)
    ).astype(jnp.bfloat16)
    pair = jnp.stack((keys[0], values[0]))
    pair_blocks = pair.reshape(2, local, BLOCK, width)
    outgoing = jnp.einsum(
        "rcu,xubw->rcxbw", table, pair_blocks, preferred_element_type=jnp.float32
    ).astype(jnp.bfloat16)
    incoming = lax.all_to_all(outgoing, "seq", split_axis=0, concat_axis=0, tiled=True)
    random_tiles = incoming.reshape(flat_slots, 2, BLOCK, width)[my_positions]
    random_tiles = jnp.moveaxis(random_tiles.reshape(local, RANDOM, 2, BLOCK, width), 2, 0)
    padded = extended(pair, (("seq", 1),), BLOCK).reshape(2, local + 2, BLOCK, width)
    window = jnp.stack(
        (padded[:, 0:local], padded[:, 1 : local + 1], padded[:, 2 : local + 2]), axis=2
    )
    anchor = spread(pair, "seq", 0).reshape(2, 1, 2, BLOCK, width)
    anchor_tiles = jnp.broadcast_to(anchor, (2, local, 2, BLOCK, width))
    tiles = jnp.concatenate((window, anchor_tiles, random_tiles), axis=2)
    rows = seq_index * local + jnp.arange(local, dtype=jnp.int32)
    block_ids, valid = slot_table(rows, random_blocks[0], total)
    mask = jnp.repeat(valid, BLOCK, axis=1)
    grad_attn = jnp.einsum(
        "tw,rw->tr",
        grad_out[0],
        lax.all_gather(proj, "dp", axis=0, tiled=True),
        preferred_element_type=jnp.float32,
    ).astype(jnp.bfloat16)
    query_heads = queries[0].reshape(local, BLOCK, HEADS, HEAD_DIM)
    grad_heads = grad_attn.reshape(local, BLOCK, HEADS, HEAD_DIM)
    key_heads = tiles[0].reshape(local, count * BLOCK, HEADS, HEAD_DIM)
    value_heads = tiles[1].reshape(local, count * BLOCK, HEADS, HEAD_DIM)
    scores = (
        jnp.einsum("qahd,qkhd->qhak", query_heads, key_heads, preferred_element_type=jnp.float32)
        * scale
    )
    scores = jnp.where(mask[:, None, None, :], scores, -jnp.inf)
    top = jnp.max(scores, axis=3, keepdims=True)
    lse = top + jnp.log(jnp.sum(jnp.exp(scores - top), axis=3, keepdims=True))
    prob = jnp.exp(scores - lse)
    prob_low = prob.astype(jnp.bfloat16)
    attn = jnp.einsum(
        "qhak,qkhd->qahd", prob_low, value_heads, preferred_element_type=jnp.float32
    ).astype(jnp.bfloat16)
    delta = jnp.sum(grad_heads.astype(jnp.float32) * attn.astype(jnp.float32), axis=3)
    delta = jnp.transpose(delta, (0, 2, 1))[..., None]
    dprob = jnp.einsum(
        "qahd,qkhd->qhak", grad_heads, value_heads, preferred_element_type=jnp.float32
    )
    dscore = (scale * prob * (dprob - delta)).astype(jnp.bfloat16)
    grad_q = jnp.einsum("qhak,qkhd->qahd", dscore, key_heads, preferred_element_type=jnp.float32)
    grad_queries = grad_q.reshape(1, tokens, width).astype(jnp.bfloat16)
    key_terms = jnp.einsum(
        "qhak,qahd->qkhd", dscore, query_heads, preferred_element_type=jnp.float32
    )
    value_terms = jnp.einsum(
        "qhak,qahd->qkhd", prob_low, grad_heads, preferred_element_type=jnp.float32
    )
    terms = jnp.stack((key_terms, value_terms)).reshape(2, local, count, BLOCK, width)
    live = valid.astype(jnp.float32)[None, :, :, None, None]
    rounded = (terms * live).astype(jnp.bfloat16)
    empty_tile = jnp.zeros((2, 1, BLOCK, width), jnp.float32)
    accum = jnp.concatenate((empty_tile, terms[:, :, 1], empty_tile), axis=1)
    accum = accum + jnp.concatenate(
        (rounded[:, :, 0].astype(jnp.float32), empty_tile, empty_tile), axis=1
    )
    accum = accum + jnp.concatenate(
        (empty_tile, empty_tile, rounded[:, :, 2].astype(jnp.float32)), axis=1
    )
    edges = jnp.concatenate((accum[:, 0], accum[:, local + 1]), axis=1).astype(jnp.bfloat16)
    edge_back = extended(edges, (("seq", 1),), BLOCK)
    inner = accum[:, 1 : local + 1]
    inner = inner.at[:, 0].add(edge_back[:, 0:BLOCK].astype(jnp.float32))
    inner = inner.at[:, local - 1].add(edge_back[:, 3 * BLOCK : 4 * BLOCK].astype(jnp.float32))
    anchor_part = jnp.sum(rounded[:, :, 3:5].astype(jnp.float32), axis=1)
    anchor_sum = lax.psum(anchor_part.astype(jnp.bfloat16), "seq").astype(jnp.float32)
    is_first = (seq_index == 0).astype(jnp.float32)
    inner = inner.at[:, 0:2].add(anchor_sum * is_first)
    place = (my_positions[None, :] == jnp.arange(flat_slots, dtype=jnp.int32)[:, None]).astype(
        jnp.bfloat16
    )
    back = jnp.moveaxis(rounded[:, :, 5:], 0, 2).reshape(requests, 2, BLOCK, width)
    sending = jnp.einsum("pj,jxbw->pxbw", place, back, preferred_element_type=jnp.float32).astype(
        jnp.bfloat16
    )
    sending = sending.reshape(seq_count, capacity, 2, BLOCK, width)
    returned = lax.all_to_all(sending, "seq", split_axis=0, concat_axis=0, tiled=True)
    received_terms = jnp.einsum(
        "rcu,rcxbw->xubw", table, returned, preferred_element_type=jnp.float32
    )
    grad_pair = inner + received_terms
    grad_keys = grad_pair[0].reshape(1, tokens, width).astype(jnp.bfloat16)
    grad_values = grad_pair[1].reshape(1, tokens, width).astype(jnp.bfloat16)
    attn_flat = attn.reshape(tokens, width)
    partial_rows = lax.psum_scatter(
        jnp.einsum("tr,tw->rw", attn_flat, grad_out[0], preferred_element_type=jnp.float32).astype(
            jnp.bfloat16
        ),
        "dp",
        scatter_dimension=0,
        tiled=True,
    )
    grad_proj = lax.psum(partial_rows, "seq").astype(jnp.float32)
    return (grad_queries, grad_keys, grad_values, grad_proj)


def solution(mesh):
    return jax.shard_map(
        per_device,
        mesh=mesh,
        in_specs=(
            P("dp", "seq", None),
            P("dp", "seq", None),
            P("dp", "seq", None),
            P("dp", "seq", None),
            P("dp", "seq", None),
            P("dp", None),
        ),
        out_specs=(P("dp", "seq", None), P("dp", "seq", None), P("dp", "seq", None), P("dp", None)),
        check_vma=False,
    )
```

profile of v0, /device:TPU:1, one launch (start us, length us, event | category | flops | bytes accessed | tf_op | source)
XLA Modules:
  0.0 582.4 jit_solution(5998700294587908490)
XLA Ops:
  8.1 24.7 %all_gather.6 = s32[1,32,3]{2,0,1:T(1,128)S(1)} all-gather(s32[1,2,3]{2,0,1:T(1,128)} %bitcast.140), channel_id=1, replica_groups=mesh['dp'=32,'seq'=16] {'seq'}, dimensions={1}, use_global_device_ids=true | all-gather | bytes 408 | tf_op jit(solution)/shard_map/all_gather | solution.py:63
  36.6 2.5 copy.132
  39.2 3.8 all-to-all-start
  43.1 2.1 collective-permute-start.1
  45.2 3.4 collective-permute-start
  50.0 42.3 %all_gather.7 = bf16[512,512]{1,0:T(8,128)(2,1)S(1)} all-gather(bf16[16,512]{1,0:T(8,128)(2,1)S(1)} %copy-done.7), channel_id=1, replica_groups=mesh['dp'=32,'seq'=16] {'dp'}, dimensions={0}, use_global_device_ids=true | all-gather | bytes 540672 | tf_op jit(solution)/shard_map/all_gather | solution.py:102
  98.9 78.9 %all-reduce.5.cloned.1.call-done = bf16[2,2,64,512]{3,2,1,0:T(8,128)(2,1)} async-done(((bf16[2,2,64,512]{3,2,1,0:T(8,128)(2,1)}), bf16[2,2,64,512]{3,2,1,0:T(8,128)(2,1)}) %all-reduce.5.cloned.1.call-update) | async-done | bytes 262160 | tf_op jit(solution)/shard_map/psum | solution.py:31
  177.8 1.8 broadcast_dynamic-update-slice_fusion
  181.1 2.7 fusion.44
  185.0 1.4 copy.142
  186.4 3.9 reshape_squeeze.17
  190.3 2.6 copy.139
  194.2 1.8 convolution_bitcast_fusion.1
  197.3 1.8 multiply_convert_fusion
  199.1 4.4 reshape.483
  203.5 2.9 copy.149
  206.4 3.0 convolution_bitcast_fusion
  209.4 4.4 reshape.482
  213.7 3.8 copy.148
  217.6 2.2 fusion.1
  221.5 2.5 copy.156
  223.9 6.6 %all-to-all-start.1 = ((bf16[16,1,2,64,512]{4,3,2,1,0:T(8,128)(2,1)}), bf16[16,1,2,64,512]{4,3,2,1,0:T(8,128)(2,1)}, u32[]{:S(2)}, u32[]{:S(2)}) async-start(bf16[16,1,2,64,512]{4,3,2,1,0:T(8,128)(2,1)} %copy.156), calls=%async_computation.1 | async-start | bytes 4194304 | tf_op jit(solution)/shard_map/all_to_all | solution.py:163
  234.1 1.6 fusion.13
  238.8 3.5 collective-permute-start.2
  242.3 1.9 collective-permute-start.3
  245.3 32.4 %collective-permute-done.2 = bf16[2,64,512]{2,1,0:T(8,128)(2,1)S(1)} collective-permute-done((bf16[2,64,512]{2,1,0:T(8,128)(2,1)S(1)}, bf16[2,64,512]{2,1,0:T(8,128)(2,1)S(1)}, u32[]{:S(2)}, u32[]{:S(2)}) %collective-permute-start.2) | collective-permute-done | bytes 131104 | tf_op jit(solution)/shard_map/ppermute | solution.py:20
  277.8 2.2 collective-permute-done.3
  280.7 2.4 scatter-add.9
  283.2 167.0 %reduce-scatter.2.cloned.1.call-done = bf16[16,512]{1,0:T(8,128)(2,1)} async-done(((bf16[512,512]{1,0:T(8,128)(2,1)}), bf16[16,512]{1,0:T(8,128)(2,1)}) %reduce-scatter.2.cloned.1.call-update) | async-done | bytes 16400 | tf_op jit(solution)/shard_map/reduce_scatter | solution.py:171
  450.2 49.0 %psum.23 = bf16[16,512]{1,0:T(8,128)(2,1)S(1)} all-reduce(bf16[16,512]{1,0:T(8,128)(2,1)} %reduce-scatter.2.cloned.1.call-done), channel_id=1, replica_groups=mesh['dp'=32,'seq'=16] {'seq'}, use_global_device_ids=true, to_apply=%region_10.11 | all-reduce | flops 8192 | bytes 32768 | tf_op jit(solution)/shard_map/psum | solution.py:179
  499.9 71.4 %all-reduce.7.cloned.1.call-done = bf16[2,2,64,512]{3,1,2,0:T(2,128)(2,1)} async-done(((bf16[2,2,64,512]{3,1,2,0:T(2,128)(2,1)}), bf16[2,2,64,512]{3,1,2,0:T(2,128)(2,1)}) %all-reduce.7.cloned.1.call-update) | async-done | bytes 262160 | tf_op jit(solution)/shard_map/psum | solution.py:152
  571.3 3.1 add_convert_fusion
  (106 shorter events, 29.9 us)
Async XLA Ops:
  7.2 85.2 %copy-start = (bf16[1,128,512]{2,1,0:T(8,128)(2,1)S(1)}, bf16[1,128,512]{2,1,0:T(8,128)(2,1)}, u32[]{:S(2)}) copy-start(bf16[1,128,512]{2,1,0:T(8,128)(2,1)} %param.17) | copy-start | bytes 393220
  39.2 10.5 %copy-start.8 = (s32[1,2,3]{2,1,0:T(2,128)S(1)}, s32[1,2,3]{2,1,0:T(2,128)}, u32[]{:S(2)}) copy-start(s32[1,2,3]{2,1,0:T(2,128)} %param.18) | copy-start | bytes 76
  39.2 10.8 %copy-start.7 = (bf16[16,512]{1,0:T(8,128)(2,1)S(1)}, bf16[16,512]{1,0:T(8,128)(2,1)}, u32[]{:S(2)}) copy-start(bf16[16,512]{1,0:T(8,128)(2,1)} %param.19) | copy-start | bytes 49156
  39.2 140.4 %all-to-all-start = ((bf16[16,1,2,64,512]{4,3,2,1,0:T(8,128)(2,1)}), bf16[16,1,2,64,512]{4,3,2,1,0:T(8,128)(2,1)S(1)}, u32[]{:S(2)}, u32[]{:S(2)}) async-start(bf16[16,1,2,64,512]{4,3,2,1,0:T(8,128)(2,1)} %copy.132), calls=%async_computation | async-start | bytes 4194304 | tf_op jit(solution)/shard_map/all_to_all | solution.py:86
  43.0 50.2 %copy-start.6 = (bf16[1,128,512]{2,1,0:T(8,128)(2,1)S(1)}, bf16[1,128,512]{2,1,0:T(8,128)(2,1)}, u32[]{:S(2)}) copy-start(bf16[1,128,512]{2,1,0:T(8,128)(2,1)} %param.14) | copy-start | bytes 393220
  43.0 134.7 %all-reduce.5.cloned.1.call-start = ((), (), s32[]{:S(2)}) async-start(), calls=%async_computation.3 | async-start | bytes 524288 | tf_op jit(solution)/shard_map/psum | solution.py:31
  43.1 52.5 %collective-permute-start.1 = (bf16[2,64,512]{2,1,0:T(8,128)(2,1)S(1)}, bf16[2,64,512]{2,1,0:T(8,128)(2,1)}, u32[]{:S(2)}, u32[]{:S(2)}) collective-permute-start(bf16[2,64,512]{2,1,0:T(8,128)(2,1)S(1)} %get-tuple-element.64), channel_id=1, source_target_pairs={{1,0},{2,1},{3,2},{4,3},{5,4},{6,5},{7,6},{8,7},{9,8},{10,9},{11,1... | collective-permute-start | bytes 393224 | tf_op jit(solution)/shard_map/ppermute | solution.py:22
  45.2 50.4 %collective-permute-start = (bf16[2,64,512]{2,1,0:T(8,128)(2,1)S(1)}, bf16[2,64,512]{2,1,0:T(8,128)(2,1)}, u32[]{:S(2)}, u32[]{:S(2)}) collective-permute-start(bf16[2,64,512]{2,1,0:T(8,128)(2,1)S(1)} %get-tuple-element.63), channel_id=1, source_target_pairs={{0,1},{1,2},{2,3},{3,4},{4,5},{5,6},{6,7},{7,8},{8,9},{9,10},{10,1... | collective-permute-start | bytes 393224 | tf_op jit(solution)/shard_map/ppermute | solution.py:20
  49.6 43.1 %copy-start.9 = (s32[6]{0:T(128)}, s32[6]{0:T(128)S(1)}, u32[]{:S(2)}) copy-start(s32[6]{0:T(128)S(1)} %dynamic-slice_reduce_fusion) | copy-start | bytes 76
  190.3 2.6 copy-start.3
  203.5 2.9 copy-start.4
  219.8 1.6 copy-start.1
  219.8 0.7 copy-start.10
  223.9 6.7 %copy-start.5 = (bf16[2,64,8,64]{1,3,2,0:T(8,128)(2,1)S(1)}, bf16[2,64,8,64]{1,3,2,0:T(8,128)(2,1)}, u32[]{:S(2)}) copy-start(bf16[2,64,8,64]{1,3,2,0:T(8,128)(2,1)} %get-tuple-element.70) | copy-start | bytes 393220
  223.9 347.4 %all-to-all-start.1 = ((bf16[16,1,2,64,512]{4,3,2,1,0:T(8,128)(2,1)}), bf16[16,1,2,64,512]{4,3,2,1,0:T(8,128)(2,1)}, u32[]{:S(2)}, u32[]{:S(2)}) async-start(bf16[16,1,2,64,512]{4,3,2,1,0:T(8,128)(2,1)} %copy.156), calls=%async_computation.1 | async-start | bytes 4194304 | tf_op jit(solution)/shard_map/all_to_all | solution.py:163
  230.5 219.7 %reduce-scatter.2.cloned.1.call-start = ((), (), s32[]{:S(2)}) async-start(), calls=%async_computation.5 | async-start | bytes 540672 | tf_op jit(solution)/shard_map/reduce_scatter | solution.py:171
  233.8 337.5 %all-reduce.7.cloned.1.call-start = ((), (), s32[]{:S(2)}) async-start(), calls=%async_computation.4 | async-start | bytes 524288 | tf_op jit(solution)/shard_map/psum | solution.py:152
  236.8 1.7 copy-start.2
  238.8 38.9 %collective-permute-start.2 = (bf16[2,64,512]{2,1,0:T(8,128)(2,1)S(1)}, bf16[2,64,512]{2,1,0:T(8,128)(2,1)S(1)}, u32[]{:S(2)}, u32[]{:S(2)}) collective-permute-start(bf16[2,64,512]{2,1,0:T(8,128)(2,1)S(1)} %get-tuple-element.57), channel_id=1, source_target_pairs={{0,1},{1,2},{2,3},{3,4},{4,5},{5,6},{6,7},{7,8},{8,9},{9,10},{10,1... | collective-permute-start | bytes 393224 | tf_op jit(solution)/shard_map/ppermute | solution.py:20
  242.3 37.6 %collective-permute-start.3 = (bf16[2,64,512]{2,1,0:T(8,128)(2,1)S(1)}, bf16[2,64,512]{2,1,0:T(8,128)(2,1)S(1)}, u32[]{:S(2)}, u32[]{:S(2)}) collective-permute-start(bf16[2,64,512]{2,1,0:T(8,128)(2,1)S(1)} %get-tuple-element.56), channel_id=1, source_target_pairs={{1,0},{2,1},{3,2},{4,3},{5,4},{6,5},{7,6},{8,7},{9,8},{10,9},{11,1... | collective-permute-start | bytes 393224 | tf_op jit(solution)/shard_map/ppermute | solution.py:22
Sparse Core Ops, SparseCore 0:
  49.5 128.1 all-reduce.4
  236.4 213.7 reduce-scatter.1
  452.5 118.7 all-reduce.6
where the time goes:
time: 583 us; the launch traced here: 582 us
  waiting for transfers between devices  352 us (60%)
  blocking collectives  116 us (20%)
  local copies, waits for them, and re-layouts  52.4 us (9%)
  starting transfers between devices  21.8 us (4%)
  matrix products  16.3 us (3%)
  between operations  14.2 us (2%)
  other arithmetic  9.58 us (2%)
    reduce_scatter x1, waiting for transfers between devices, per_device(): lax.psum_scatter(jnp.einsum('tr,tw->rw', attn_flat, grad_out[0], preferre...  167 us
    psum x1, waiting for transfers between devices, spread(): return lax.psum(kept, axis)  78.9 us
    psum x1, waiting for transfers between devices, per_device(): lax.psum(anchor_part.astype(jnp.bfloat16), 'seq').astype(jnp.float32)  71.4 us
    psum x1, blocking collectives, per_device(): grad_proj = lax.psum(partial_rows, 'seq').astype(jnp.float32)  49 us
    all_gather x1, blocking collectives, per_device(): lax.all_gather(proj, 'dp', axis=0, tiled=True)  42.3 us
    ppermute x2, waiting for transfers between devices, extended(): lax.ppermute(tail, axis, [(i, (i + 1) % count) for i in range(ends)])  32.4 us
    all_gather x1, blocking collectives, per_device(): lists = lax.all_gather(random_blocks, 'seq', axis=1, tiled=True)[0]  24.7 us
    another operation x4, local copies, waits for them, and re-layouts, per_device(): jnp.stack((key_terms, value_terms)).reshape(2, local, count, BLOCK, width)  15.5 us
  transfers between devices with their start and end apart: 9, of which 5 were waited for; matrix products, arithmetic and copies ran while one was open for 4% of the time, Pallas kernels for 0%

commit v1 on v0

v1 whole, which is shorter than its diff:
```python
import functools

import jax
import jax.numpy as jnp
from jax import lax
from jax.experimental import pallas as pl
from jax.experimental.pallas import tpu as pltpu
from jax.sharding import PartitionSpec as P

HEADS = 8
HEAD_DIM = 64
BLOCK = 64
RANDOM = 3
CHIPS = 8
TOKENS = 128
WIDTH = 512
HALF = 256
BLOCKS = 32
SCALE = HEAD_DIM ** (-0.5)
NEG = -1e30
NEAR = (1, 7, 2, 6, 3, 5, 4)
FAR = (4, 3, 5, 2, 6, 1, 7)

TBL, KV, KVF, QS, GS, PX, PY, PS = 0, 8, 16, 24, 32, 40, 44, 52
DQ, XK, DK, RS, RX, RY, RZ, RF = 56, 64, 72, 80, 84, 88, 96, 104
SEMS = 112


def dot(a, b, dims):
    return lax.dot_general(a, b, (dims, ((), ())), preferred_element_type=jnp.float32)


def kernel(nx, ny, q_ref, k_ref, v_ref, go_ref, rb_ref, pj_ref, gq_ref, gk_ref, gv_ref, gp_ref,
           tblme, tblv, tbls, kvp, kv, qp, qr, gpk, gr, pj, acc, trand, dqs, dqr, xs, xr, dks, dkr,
           pp, pps, s1, rx, s2, ry, s3, rz, s4, s4b, ssem, rsem, lsem):
    dp = lax.axis_index("dp")
    s = lax.axis_index("seq")
    z, c = s // 2, s % 2
    y, x = dp // nx, dp % nx
    other = 1 - c
    sib = (dp, 2 * z + other)
    rows = nx * ny * 16

    def zdev(zt):
        return (dp, 2 * zt + c)

    def send(src, dst, sem, dev):
        copy = pltpu.make_async_remote_copy(
            src_ref=src, dst_ref=dst, send_sem=ssem.at[sem], recv_sem=rsem.at[sem],
            device_id=dev, device_id_type=pl.DeviceIdType.MESH)
        copy.start()

    def got(dst, sem):
        pltpu.make_async_remote_copy(
            src_ref=dst, dst_ref=dst, send_sem=ssem.at[sem], recv_sem=rsem.at[sem],
            device_id=sib, device_id_type=pl.DeviceIdType.MESH).wait_recv()

    def sent(src, sem):
        pltpu.make_async_remote_copy(
            src_ref=src, dst_ref=src, send_sem=ssem.at[sem], recv_sem=rsem.at[sem],
            device_id=sib, device_id_type=pl.DeviceIdType.MESH).wait_send()

    def ahead(off):
        return (z + off) % CHIPS

    def behind(off):
        return (z + CHIPS - off) % CHIPS

    barrier = pltpu.get_barrier_semaphore()
    partners = [sib] + [zdev(ahead(off)) for off in range(1, CHIPS)]
    partners += [(y * nx + (x + d) % nx, s) for d in range(1, nx)]
    partners += [(((y + d) % ny) * nx + x, s) for d in range(1, ny)]
    for dev in partners:
        pl.semaphore_signal(barrier, inc=1, device_id=dev, device_id_type=pl.DeviceIdType.MESH)
    pl.semaphore_wait(barrier, len(partners))

    mine = pl.ds(pl.multiple_of(c * HALF, HALF), HALF)
    theirs = pl.ds(pl.multiple_of(other * HALF, HALF), HALF)

    with jax.named_scope("proj_rows_x"):
        own_rows = pl.ds(pl.multiple_of(dp * 16, 16), 16)
        for d in range(1, nx):
            send(pj_ref.at[:, mine], pj.at[c, own_rows], PX + d, (y * nx + (x + d) % nx, s))
        pj[c, own_rows] = pj_ref[:, mine]

    with jax.named_scope("key_value_blocks"):
        lane = lax.broadcasted_iota(jnp.int32, (8, 128), 1)
        row = jnp.zeros((8, 128), jnp.int32)
        for e in range(2 * RANDOM):
            block = rb_ref[0, e // RANDOM, e % RANDOM]
            own = block // 2
            row = jnp.where(lane == own, e, row)
            row = jnp.where(lane == own + 16 + 16 * (block % 2), 1, row)
            row = jnp.where(lane == 48 + e, block, row)
        tblme[...] = row
        tblv[z] = row
        for off in NEAR:
            send(tblme, tblv.at[z], TBL + off, zdev(ahead(off)))
        for h in range(HEADS):
            f = slice(h * HEAD_DIM, (h + 1) * HEAD_DIM)
            packed = jnp.concatenate([k_ref[0, :, f], v_ref[0, :, f]], axis=1)
            kvp[h] = packed.reshape(2, BLOCK, 128)
        kv[pl.ds(2 * s, 2)] = kvp[z]
        for off in FAR:
            zt = ahead(off)
            send(kvp.at[zt], kv.at[pl.ds(2 * s, 2)], KV + off, zdev(zt))
        send(kvp.at[z], kv.at[pl.ds(2 * s, 2)], KVF, sib)

    with jax.named_scope("query_blocks"):
        for h in range(HEADS):
            f = slice(h * HEAD_DIM, (h + 1) * HEAD_DIM)
            qp[h] = jnp.concatenate([q_ref[0, :BLOCK, f], q_ref[0, BLOCK:, f]], axis=1)
        qr[z] = qp[z]
        for off in FAR:
            zt = ahead(off)
            send(qp.at[zt], qr.at[z], QS + off, zdev(zt))

    with jax.named_scope("proj_rows_y"):
        group = nx * 16
        own_group = pl.ds(pl.multiple_of(y * group, group), group)
        for d in range(1, nx):
            xf = (x + nx - d) % nx
            got(pj.at[c, pl.ds(pl.multiple_of((y * nx + xf) * 16, 16), 16)], PX + d)
        for d in range(1, ny):
            send(pj.at[c, own_group], pj.at[c, own_group], PY + d, (((y + d) % ny) * nx + x, s))

    acc[...] = jnp.zeros_like(acc)

    with jax.named_scope("proj_rows_y_wait"):
        for d in range(1, ny):
            yf = (y + ny - d) % ny
            got(pj.at[c, pl.ds(pl.multiple_of(yf * group, group), group)], PY + d)
        send(pj.at[c], pj.at[c], PS, sib)

    def forward(off):
        zf = behind(off)
        part = kv.at[pl.ds(4 * zf + 2 * c, 2)]
        got(part, KV + off)
        send(part, part, KVF + off, sib)

    for off in NEAR[:4]:
        forward(off)

    with jax.named_scope("grad_attn"):
        got(pj.at[other], PS)
        ga = dot(go_ref[0, :, :HALF], pj[0], ((1,), (1,)))
        ga += dot(go_ref[0, :, HALF:], pj[1], ((1,), (1,)))
        ga = ga.astype(jnp.bfloat16)
        for h in range(HEADS):
            f = slice(h * HEAD_DIM, (h + 1) * HEAD_DIM)
            gpk[h] = jnp.concatenate([ga[:BLOCK, f], ga[BLOCK:, f]], axis=1)
        gr[z] = gpk[z]
        for off in FAR:
            zt = ahead(off)
            send(gpk.at[zt], gr.at[z], GS + off, zdev(zt))

    for off in NEAR[4:]:
        forward(off)
    for off in NEAR:
        got(tblv.at[behind(off)], TBL + off)
    table = pltpu.make_async_copy(tblv, tbls, lsem.at[0])
    table.start()
    table.wait()
    for off in (0,) + NEAR:
        got(kv.at[pl.ds(4 * behind(off) + 2 * other, 2)], KVF + off)

    slot = lax.broadcasted_iota(jnp.int32, (1, 8 * BLOCK), 1) // BLOCK
    low = lax.broadcasted_iota(jnp.int32, (BLOCK, 128), 1) < HEAD_DIM

    def attend(zs, b, qf, gf):
        i = 4 * zs + 2 * c + b
        before, after = jnp.maximum(i - 1, 0), jnp.minimum(i + 1, BLOCKS - 1)
        ids = [tbls[zs, 0, 48 + RANDOM * b + n] for n in range(RANDOM)]
        valid = [i >= 1, i >= 0, i < BLOCKS - 1, i >= 2, i >= 3]
        for n in range(RANDOM):
            r = ids[n]
            clash = (r == i - 1) | (r == i) | (r == i + 1) | (r <= 1)
            for earlier in ids[:n]:
                clash = clash | (r == earlier)
            valid.append(jnp.logical_not(clash))
        bias = jnp.zeros((1, 8 * BLOCK), jnp.float32)
        for n in range(8):
            bias = jnp.where(slot == n, jnp.where(valid[n], 0.0, NEG), bias)
        tiles = jnp.concatenate(
            [kv[before], kv[i], kv[after], kv[0], kv[1]] + [kv[r] for r in ids], axis=0)
        if b == 0:
            gf = jnp.concatenate([gf[:, HEAD_DIM:], gf[:, :HEAD_DIM]], axis=1)
        else:
            qf = jnp.concatenate([qf[:, HEAD_DIM:], qf[:, :HEAD_DIM]], axis=1)
        zero = jnp.zeros_like(qf)
        ql = jnp.where(low, qf, zero)
        gl = jnp.where(low, zero, gf)
        both = dot(jnp.concatenate([ql, gl], axis=0), tiles, ((1,), (1,)))
        scores = both[:BLOCK] * SCALE + bias
        dprob = both[BLOCK:]
        top = jnp.max(scores, axis=1, keepdims=True)
        e = jnp.exp(scores - top)
        prob = e * (1.0 / jnp.sum(e, axis=1, keepdims=True))
        delta = jnp.sum(prob * dprob, axis=1, keepdims=True)
        dscore = prob * (dprob - delta) * SCALE
        pd = jnp.concatenate([prob, dscore], axis=0).astype(jnp.bfloat16)
        out = dot(pd, tiles, ((1,), (0,)))
        terms = dot(pd, jnp.concatenate([gl, ql], axis=0), ((0,), (0,)))
        for n, j in enumerate((before, i, after, 0, 1)):
            acc[j] += terms[n * BLOCK:(n + 1) * BLOCK]
        for n in range(RANDOM):
            trand[zs * 2 * RANDOM + RANDOM * b + n] = terms[(5 + n) * BLOCK:(6 + n) * BLOCK]
        dqs[zs, b] = jnp.where(low, out[BLOCK:], out[:BLOCK]).astype(jnp.bfloat16)

    def offset(step):
        odd = step % 2
        return (odd * ((step + 1) // 2) + (1 - odd) * (CHIPS - step // 2)) % CHIPS

    with jax.named_scope("attention"):
        @pl.loop(0, CHIPS)
        def _(step):
            off = offset(step)
            zs = behind(off)

            @pl.when(step > 0)
            def _():
                got(qr.at[zs], QS + off)
                got(gr.at[zs], GS + off)

            qf, gf = qr[zs], gr[zs]
            for b in range(2):
                attend(zs, b, qf, gf)

            @pl.when(step > 0)
            def _():
                send(dqs.at[zs], dqr.at[z], DQ + off, zdev(zs))

        dqr[z] = dqs[z]

    def pull(o):
        parts = [acc[2 * o], acc[2 * o + 1]]
        for zs in range(CHIPS):
            term = trand[zs * 2 * RANDOM + tbls[zs, 0, o]]
            for w in range(2):
                parts[w] += term * tbls[zs, 0, 16 + 16 * w + o].astype(jnp.float32)
        return parts

    with jax.named_scope("other_core_terms"):
        @pl.loop(0, CHIPS)
        def _(k):
            parts = pull(2 * k + other)
            for w in range(2):
                xs[k, w] = parts[w].astype(jnp.bfloat16)
            send(xs.at[k], xr.at[k], XK + k, sib)

    with jax.named_scope("partial_proj"):
        for off in NEAR:
            got(dqr.at[ahead(off)], DQ + off)
        pieces = [dqr[h].reshape(TOKENS, 128) for h in range(HEADS)]
        attn = jnp.concatenate([p[:, HEAD_DIM:] for p in pieces], axis=1)
        for half in range(2):
            f = slice(half * HALF, (half + 1) * HALF)
            pp[half] = dot(attn, go_ref[0, :, f], ((0,), (0,))).astype(jnp.bfloat16)
        send(pp.at[other], pps, RS, sib)
        gq_ref[0] = jnp.concatenate([p[:, :HEAD_DIM] for p in pieces], axis=1)

    with jax.named_scope("own_terms"):
        @pl.loop(0, CHIPS)
        def _(step):
            off = (step + 4) % CHIPS
            k = ahead(off)
            parts = pull(2 * k + c)
            got(xr.at[k], XK + k)
            for w in range(2):
                dks[k, w] = (parts[w] + xr[k, w].astype(jnp.float32)).astype(jnp.bfloat16)

            @pl.when(off > 0)
            def _():
                send(dks.at[k], dkr.at[z], DK + off, zdev(k))

        dkr[z] = dks[z]

    def wide(ref):
        return ref.astype(jnp.float32)

    with jax.named_scope("grad_proj_x"):
        got(pps, RS)
        s1[...] = (wide(pp[c]) + wide(pps[...])).astype(jnp.bfloat16).reshape(ny, nx, 16, HALF)
        for d in range(1, nx):
            xt = (x + d) % nx
            send(s1.at[:, xt], rx.at[d], RX + d, (y * nx + xt, s))
        total = wide(s1[:, x])
        for d in range(1, nx):
            got(rx.at[d], RX + d)
            total += wide(rx[d])
        s2[...] = total.astype(jnp.bfloat16)
    with jax.named_scope("grad_proj_y"):
        for d in range(1, ny):
            yt = (y + d) % ny
            send(s2.at[yt], ry.at[d], RY + d, (yt * nx + x, s))
        total = wide(s2[y])
        for d in range(1, ny):
            got(ry.at[d], RY + d)
            total += wide(ry[d])
        s3[...] = total.astype(jnp.bfloat16)
    with jax.named_scope("grad_proj_z"):
        rz[z] = s3[...]
        for off in FAR:
            send(s3, rz.at[z], RZ + off, zdev(ahead(off)))
        for off in NEAR:
            got(rz.at[behind(off)], RZ + off)
        total = wide(rz[0])
        for k in range(1, CHIPS):
            total += wide(rz[k])
        s4[...] = total
        send(s4, s4b, RF, sib)
        gp_ref[:, mine] = total

    with jax.named_scope("grad_keys_values"):
        for off in NEAR:
            got(dkr.at[behind(off)], DK + off)
        pieces = [dkr[h].reshape(TOKENS, 128) for h in range(HEADS)]
        gk_ref[0] = jnp.concatenate([p[:, :HEAD_DIM] for p in pieces], axis=1)
        gv_ref[0] = jnp.concatenate([p[:, HEAD_DIM:] for p in pieces], axis=1)

    got(s4b, RF)
    gp_ref[:, theirs] = s4b[...]

    with jax.named_scope("sent"):
        for d in range(1, nx):
            sent(pj_ref.at[:, mine], PX + d)
            sent(s1.at[:, (x + d) % nx], RX + d)
        for d in range(1, ny):
            sent(pj.at[c, own_group], PY + d)
            sent(s2.at[(y + d) % ny], RY + d)
        sent(pj.at[c], PS)
        sent(pp.at[other], RS)
        sent(s4, RF)
        sent(kvp.at[z], KVF)
        sent(xs.at[0], XK)
        for off in range(1, CHIPS):
            zt, zf = ahead(off), behind(off)
            sent(tblme, TBL + off)
            sent(kvp.at[zt], KV + off)
            sent(kv.at[pl.ds(4 * zf + 2 * c, 2)], KVF + off)
            sent(qp.at[zt], QS + off)
            sent(gpk.at[zt], GS + off)
            sent(dqs.at[zf], DQ + off)
            sent(xs.at[off], XK + off)
            sent(dks.at[zt], DK + off)
            sent(s3, RZ + off)


def attention_grads(nx, ny, q, k, v, go, rb, proj):
    bf, f32 = jnp.bfloat16, jnp.float32
    rows = nx * ny * 16
    vmem = pl.BlockSpec(memory_space=pltpu.VMEM)
    smem = pl.BlockSpec(memory_space=pltpu.SMEM)
    scratch = [
        pltpu.VMEM((8, 128), jnp.int32),
        pltpu.VMEM((CHIPS, 8, 128), jnp.int32),
        pltpu.SMEM((CHIPS, 8, 128), jnp.int32),
        pltpu.VMEM((HEADS, 2, BLOCK, 128), bf),
        pltpu.VMEM((BLOCKS, BLOCK, 128), bf),
        pltpu.VMEM((HEADS, BLOCK, 128), bf),
        pltpu.VMEM((CHIPS, BLOCK, 128), bf),
        pltpu.VMEM((HEADS, BLOCK, 128), bf),
        pltpu.VMEM((CHIPS, BLOCK, 128), bf),
        pltpu.VMEM((2, rows, HALF), bf),
        pltpu.VMEM((BLOCKS, BLOCK, 128), f32),
        pltpu.VMEM((CHIPS * 2 * RANDOM, BLOCK, 128), f32),
        pltpu.VMEM((CHIPS, 2, BLOCK, 128), bf),
        pltpu.VMEM((HEADS, 2, BLOCK, 128), bf),
        pltpu.VMEM((CHIPS, 2, BLOCK, 128), bf),
        pltpu.VMEM((CHIPS, 2, BLOCK, 128), bf),
        pltpu.VMEM((CHIPS, 2, BLOCK, 128), bf),
        pltpu.VMEM((HEADS, 2, BLOCK, 128), bf),
        pltpu.VMEM((2, rows, HALF), bf),
        pltpu.VMEM((rows, HALF), bf),
        pltpu.VMEM((ny, nx, 16, HALF), bf),
        pltpu.VMEM((nx, ny, 16, HALF), bf),
        pltpu.VMEM((ny, 16, HALF), bf),
        pltpu.VMEM((ny, 16, HALF), bf),
        pltpu.VMEM((16, HALF), bf),
        pltpu.VMEM((CHIPS, 16, HALF), bf),
        pltpu.VMEM((16, HALF), f32),
        pltpu.VMEM((16, HALF), f32),
        pltpu.SemaphoreType.DMA((SEMS,)),
        pltpu.SemaphoreType.DMA((SEMS,)),
        pltpu.SemaphoreType.DMA((1,)),
    ]
    tokens = jax.ShapeDtypeStruct((1, TOKENS, WIDTH), bf)
    return pl.pallas_call(
        functools.partial(kernel, nx, ny),
        out_shape=[tokens, tokens, tokens, jax.ShapeDtypeStruct((16, WIDTH), f32)],
        in_specs=[vmem, vmem, vmem, vmem, smem, vmem],
        out_specs=[vmem, vmem, vmem, vmem],
        scratch_shapes=scratch,
        compiler_params=pltpu.CompilerParams(
            collective_id=0, has_side_effects=True, vmem_limit_bytes=32 * 1024 * 1024),
        cost_estimate=pl.CostEstimate(
            flops=2 * 500_000_000, bytes_accessed=2_000_000, transcendentals=600_000),
    )(q, k, v, go, rb, proj)


def solution(mesh, nx=4, ny=8):
    tokens = P("dp", "seq", None)
    return jax.shard_map(
        functools.partial(attention_grads, nx, ny),
        mesh=mesh,
        in_specs=(tokens, tokens, tokens, tokens, tokens, P("dp", None)),
        out_specs=(tokens, tokens, tokens, P("dp", None)),
        check_vma=False,
    )
```

time: 583 us -> 77.7 us (0.13)
  waiting for transfers between devices: 352 us -> 0 us
  blocking collectives: 116 us -> 0 us
  Pallas kernels: 0 us -> 69.2 us
  local copies, waits for them, and re-layouts: 52.4 us -> 7.59 us
  starting transfers between devices: 21.8 us -> 0 us
  matrix products: 16.3 us -> 0 us
  between operations: 14.2 us -> 0.66 us
  other arithmetic: 9.58 us -> 0 us
    reduce_scatter x1 -> x0, waiting for transfers between devices: 167 us -> none  [per_device(): lax.psum_scatter(jnp.einsum('tr,tw->rw', attn_flat, grad_out[0], preferre...]
    psum x2 -> x0, waiting for transfers between devices: 150 us -> none  [the longest x1 78.9 us: spread(): return lax.psum(kept, axis)]
    pallas_call x0 -> x1, Pallas kernels: none -> 69.2 us  [attention_grads(): pl.pallas_call(functools.partial(kernel, nx, ny), out_shape=[tokens, toke...]
    all_gather x2 -> x0, blocking collectives: 67.1 us -> none  [the longest x1 42.3 us: per_device(): lax.all_gather(proj, 'dp', axis=0, tiled=True)]
    psum x1 -> x0, blocking collectives: 49 us -> none  [per_device(): grad_proj = lax.psum(partial_rows, 'seq').astype(jnp.float32)]
    ppermute x4 -> x0, waiting for transfers between devices: 34.6 us -> none  [the longest x2 32.4 us: extended(): lax.ppermute(tail, axis, [(i, (i + 1) % count) for i in range(ends)])]
    another operation x17 -> x0, local copies, waits for them, and re-layouts: 26.7 us -> none  [the longest x4 15.5 us: per_device(): jnp.stack((key_terms, value_terms)).reshape(2, local, count, BLOCK, width)]
    dot_general x11 -> x0, matrix products: 16.3 us -> none  [the longest x1 3.05 us: per_device(): jnp.einsum('rcu,rcxbw->xubw', table, returned, preferred_element_type=jnp...]
  transfers between devices with their start and end apart: 9 -> 0, of which waited for: 5 -> 0; matrix products, arithmetic and copies ran while one was open for 4% -> 0% of each run, Pallas kernels for 0% -> 0%
where the time goes in v1:
time: 77.7 us; the launch traced here: 77.4 us
  Pallas kernels  69.2 us (89%)
  local copies, waits for them, and re-layouts  7.59 us (10%)
    pallas_call x1, Pallas kernels, attention_grads(): pl.pallas_call(functools.partial(kernel, nx, ny), out_shape=[tokens, toke...  69.2 us
    unnamed x16, local copies, waits for them, and re-layouts  7.59 us

profile of v1, /device:TPU:1, one launch (start us, length us, event | category | flops | bytes accessed | tf_op | source)
XLA Modules:
  0.0 77.4 jit_solution(2592931377414632500)
XLA Ops:
  0.6 0.0 copy-start
  0.6 0.9 %copy-done = bf16[1,128,512]{2,1,0:T(8,128)(2,1)S(1)} copy-done((bf16[1,128,512]{2,1,0:T(8,128)(2,1)S(1)}, bf16[1,128,512]{2,1,0:T(8,128)(2,1)}, u32[]{:S(2)}) %copy-start) | copy-done | bytes 131096
  1.5 0.0 copy-start.1
  1.5 0.9 %copy-done.1 = bf16[1,128,512]{2,1,0:T(8,128)(2,1)S(1)} copy-done((bf16[1,128,512]{2,1,0:T(8,128)(2,1)S(1)}, bf16[1,128,512]{2,1,0:T(8,128)(2,1)}, u32[]{:S(2)}) %copy-start.1) | copy-done | bytes 131096
  2.4 0.0 copy-start.2
  2.4 0.9 %copy-done.2 = bf16[1,128,512]{2,1,0:T(8,128)(2,1)S(1)} copy-done((bf16[1,128,512]{2,1,0:T(8,128)(2,1)S(1)}, bf16[1,128,512]{2,1,0:T(8,128)(2,1)}, u32[]{:S(2)}) %copy-start.2) | copy-done | bytes 131096
  3.3 0.0 copy-start.3
  3.3 0.9 %copy-done.3 = bf16[1,128,512]{2,1,0:T(8,128)(2,1)S(1)} copy-done((bf16[1,128,512]{2,1,0:T(8,128)(2,1)S(1)}, bf16[1,128,512]{2,1,0:T(8,128)(2,1)}, u32[]{:S(2)}) %copy-start.3) | copy-done | bytes 131096
  4.3 0.0 copy-start.4
  4.3 0.7 copy-done.4
  5.0 0.0 copy-start.5
  5.0 0.7 copy-done.5
  5.6 69.2 %shard_map.93 = (bf16[1,128,512]{2,1,0:T(8,128)(2,1)S(1)}, bf16[1,128,512]{2,1,0:T(8,128)(2,1)S(1)}, bf16[1,128,512]{2,1,0:T(8,128)(2,1)S(1)}, f32[16,512]{1,0:T(8,128)S(1)}) custom-call(bf16[1,128,512]{2,1,0:T(8,128)(2,1)S(1)} %copy-done, bf16[1,128,512]{2,1,0:T(8,128)(2,1)S(1)} %copy-done.1, bf16[1,128,512]{2,1,0:T(8,128)(2,1)S(1)} %copy-done.2, ...), custom_call_target="tpu_custom_call" | custom-call | flops 1000000000 | bytes 2000000 | tf_op jit(solution)/shard_map/pallas_call | solution.py:388
  74.8 0.7 copy.14
  75.5 0.7 copy.15
  76.2 0.7 copy.16
  76.8 0.6 copy.17
Async XLA Ops:
  0.6 0.9 %copy-start = (bf16[1,128,512]{2,1,0:T(8,128)(2,1)S(1)}, bf16[1,128,512]{2,1,0:T(8,128)(2,1)}, u32[]{:S(2)}) copy-start(bf16[1,128,512]{2,1,0:T(8,128)(2,1)} %q_ref.1) | copy-start | bytes 393220
  1.5 0.9 %copy-start.1 = (bf16[1,128,512]{2,1,0:T(8,128)(2,1)S(1)}, bf16[1,128,512]{2,1,0:T(8,128)(2,1)}, u32[]{:S(2)}) copy-start(bf16[1,128,512]{2,1,0:T(8,128)(2,1)} %k_ref.1) | copy-start | bytes 393220
  2.4 0.9 %copy-start.2 = (bf16[1,128,512]{2,1,0:T(8,128)(2,1)S(1)}, bf16[1,128,512]{2,1,0:T(8,128)(2,1)}, u32[]{:S(2)}) copy-start(bf16[1,128,512]{2,1,0:T(8,128)(2,1)} %v_ref.1) | copy-start | bytes 393220
  3.3 0.9 %copy-start.3 = (bf16[1,128,512]{2,1,0:T(8,128)(2,1)S(1)}, bf16[1,128,512]{2,1,0:T(8,128)(2,1)}, u32[]{:S(2)}) copy-start(bf16[1,128,512]{2,1,0:T(8,128)(2,1)} %go_ref.1) | copy-start | bytes 393220
  4.3 0.7 copy-start.4
  5.0 0.7 copy-start.5

commit v2 on v1

v2 whole, which is shorter than its diff:
```python
import functools

import jax
import jax.numpy as jnp
from jax import lax
from jax.experimental import pallas as pl
from jax.experimental.pallas import tpu as pltpu
from jax.sharding import PartitionSpec as P

HEADS = 8
HEAD_DIM = 64
BLOCK = 64
RANDOM = 3
CHIPS = 8
TOKENS = 128
WIDTH = 512
HALF = 256
BLOCKS = 32
SCALE = HEAD_DIM ** (-0.5)
NEG = -1e30
NEAR = (1, 7, 2, 6, 3, 5, 4)
FAR = (4, 3, 5, 2, 6, 1, 7)

TBL, KV, KVF, QS, GS, PY, PX, PS = 0, 8, 16, 24, 32, 40, 48, 52
AT, DQ, XK, DK, RS, RX, RY, RZ, RF = 56, 64, 72, 80, 88, 92, 96, 104, 112
SEMS = 116


def dot(a, b, dims):
    return lax.dot_general(a, b, (dims, ((), ())), preferred_element_type=jnp.float32)


def halves(a, b):
    return jnp.concatenate([a, b], axis=1)


def kernel(nx, ny, q_hbm, k_hbm, v_hbm, go_hbm, rb_hbm, pj_hbm, gq_ref, gk_ref, gv_ref, gp_ref,
           q_ref, k_ref, v_ref, go_ref, rb_ref, pj_ref,
           tblme, tblv, tbls, kvp, kv, qp, qr, gpk, gr, pj, pst, acc, trand, ats, atr, dqs, dqr,
           xs, xr, dks, dkr, pp, pps, s1, rx, s2, ry, s3, rz, s4, s4b, ssem, rsem, lsem):
    dp = lax.axis_index("dp")
    s = lax.axis_index("seq")
    z, c = s // 2, s % 2
    y, x = dp // nx, dp % nx
    other = 1 - c
    sib = (dp, 2 * z + other)

    def zdev(zt):
        return (dp, 2 * zt + c)

    def xdev(d):
        return (y * nx + (x + d) % nx, s)

    def ydev(d):
        return (((y + d) % ny) * nx + x, s)

    def send(src, dst, sem, dev):
        copy = pltpu.make_async_remote_copy(
            src_ref=src, dst_ref=dst, send_sem=ssem.at[sem], recv_sem=rsem.at[sem],
            device_id=dev, device_id_type=pl.DeviceIdType.MESH)
        copy.start()

    def got(dst, sem):
        pltpu.make_async_remote_copy(
            src_ref=dst, dst_ref=dst, send_sem=ssem.at[sem], recv_sem=rsem.at[sem],
            device_id=sib, device_id_type=pl.DeviceIdType.MESH).wait_recv()

    def sent(src, sem):
        pltpu.make_async_remote_copy(
            src_ref=src, dst_ref=src, send_sem=ssem.at[sem], recv_sem=rsem.at[sem],
            device_id=sib, device_id_type=pl.DeviceIdType.MESH).wait_send()

    def ahead(off):
        return (z + off) % CHIPS

    def behind(off):
        return (z + CHIPS - off) % CHIPS

    barrier = pltpu.get_barrier_semaphore()
    partners = [sib] + [zdev(ahead(off)) for off in range(1, CHIPS)]
    partners += [xdev(d) for d in range(1, nx)] + [ydev(d) for d in range(1, ny)]
    for dev in partners:
        pl.semaphore_signal(barrier, inc=1, device_id=dev, device_id_type=pl.DeviceIdType.MESH)

    loads = [pltpu.make_async_copy(a, b, lsem.at[1 + n]) for n, (a, b) in enumerate((
        (pj_hbm, pj_ref), (rb_hbm, rb_ref), (k_hbm, k_ref), (v_hbm, v_ref), (q_hbm, q_ref),
        (go_hbm, go_ref)))]
    for load in loads:
        load.start()

    mine = pl.ds(pl.multiple_of(c * HALF, HALF), HALF)
    theirs = pl.ds(pl.multiple_of(other * HALF, HALF), HALF)

    with jax.named_scope("pack_inputs"):
        loads[0].wait()
        loads[1].wait()
        pj[c, y, x] = pj_ref[:, mine]
        lane = lax.broadcasted_iota(jnp.int32, (8, 128), 1)
        row = jnp.zeros((8, 128), jnp.int32)
        for e in range(2 * RANDOM):
            block = rb_ref[0, e // RANDOM, e % RANDOM]
            own = block // 2
            row = jnp.where(lane == own, e, row)
            row = jnp.where(lane == own + 16 + 16 * (block % 2), 1, row)
            row = jnp.where(lane == 48 + e, block, row)
        tblme[...] = row
        tblv[z] = row
        loads[2].wait()
        loads[3].wait()
        for h in range(HEADS):
            f = slice(h * HEAD_DIM, (h + 1) * HEAD_DIM)
            kvp[h] = halves(k_ref[0, :, f], v_ref[0, :, f]).reshape(2, BLOCK, 128)
        kv[pl.ds(2 * s, 2)] = kvp[z]
        loads[4].wait()
        for h in range(HEADS):
            f = slice(h * HEAD_DIM, (h + 1) * HEAD_DIM)
            qp[h] = halves(q_ref[0, :BLOCK, f], q_ref[0, BLOCK:, f])
        qr[z] = qp[z]

    with jax.named_scope("barrier"):
        pl.semaphore_wait(barrier, len(partners))

    with jax.named_scope("first_sends"):
        for d in range(1, ny):
            send(pj_ref.at[:, mine], pj.at[c, y, x], PY + d, ydev(d))
        for off in FAR:
            zt = ahead(off)
            send(kvp.at[zt], kv.at[pl.ds(2 * s, 2)], KV + off, zdev(zt))
        send(kvp.at[z], kv.at[pl.ds(2 * s, 2)], KVF, sib)
        for off in FAR:
            send(tblme, tblv.at[z], TBL + off, zdev(ahead(off)))
        for off in FAR:
            zt = ahead(off)
            send(qp.at[zt], qr.at[z], QS + off, zdev(zt))

    acc[...] = jnp.zeros_like(acc)

    with jax.named_scope("proj_rows_y"):
        for d in range(1, ny):
            got(pj.at[c, (y + ny - d) % ny, x], PY + d)
        for d in range(1, nx):
            send(pj.at[c, :, x], pj.at[c, :, x], PX + d, xdev(d))

    def forward(off):
        zf = behind(off)
        part = kv.at[pl.ds(4 * zf + 2 * c, 2)]
        got(part, KV + off)
        send(part, part, KVF + off, sib)

    with jax.named_scope("forward_a"):
        for off in NEAR[:4]:
            forward(off)

    with jax.named_scope("proj_rows_x"):
        for d in range(1, nx):
            got(pj.at[c, :, (x + nx - d) % nx], PX + d)
        send(pj.at[c], pj.at[c], PS, sib)

    with jax.named_scope("forward_b"):
        for off in NEAR[4:]:
            forward(off)

    with jax.named_scope("proj_other"):
        got(pj.at[other], PS)
        loads[5].wait()
    with jax.named_scope("grad_attn"):
        rows = nx * ny * 16
        ga = dot(go_ref[0, :, :HALF], pj[0].reshape(rows, HALF), ((1,), (1,)))
        ga += dot(go_ref[0, :, HALF:], pj[1].reshape(rows, HALF), ((1,), (1,)))
        ga = ga.astype(jnp.bfloat16)
        for h in range(HEADS):
            f = slice(h * HEAD_DIM, (h + 1) * HEAD_DIM)
            gpk[h] = halves(ga[:BLOCK, f], ga[BLOCK:, f])
        gr[z] = gpk[z]
        for off in FAR:
            zt = ahead(off)
            send(gpk.at[zt], gr.at[z], GS + off, zdev(zt))

    with jax.named_scope("tables"):
        for off in NEAR:
            got(tblv.at[behind(off)], TBL + off)
        table = pltpu.make_async_copy(tblv, tbls, lsem.at[0])
        table.start()
        table.wait()
    with jax.named_scope("other_core_keys"):
        for off in (0,) + NEAR:
            got(kv.at[pl.ds(4 * behind(off) + 2 * other, 2)], KVF + off)

    slot = lax.broadcasted_iota(jnp.int32, (1, 8 * BLOCK), 1) // BLOCK
    low = lax.broadcasted_iota(jnp.int32, (BLOCK, 128), 1) < HEAD_DIM

    def swap(a):
        return halves(a[:, HEAD_DIM:], a[:, :HEAD_DIM])

    def slots(zs, b):
        i = 4 * zs + 2 * c + b
        fixed = (jnp.maximum(i - 1, 0), i, jnp.minimum(i + 1, BLOCKS - 1), 0, 1)
        return i, fixed, [tbls[zs, 0, 48 + RANDOM * b + n] for n in range(RANDOM)]

    def tiles_of(fixed, ids):
        return jnp.concatenate([kv[j] for j in fixed] + [kv[r] for r in ids], axis=0)

    def softmax(zs, b, ql):
        i, fixed, ids = slots(zs, b)
        valid = [i >= 1, i >= 0, i < BLOCKS - 1, i >= 2, i >= 3]
        for n in range(RANDOM):
            r = ids[n]
            clash = (r == i - 1) | (r == i) | (r == i + 1) | (r <= 1)
            for earlier in ids[:n]:
                clash = clash | (r == earlier)
            valid.append(jnp.logical_not(clash))
        bias = jnp.zeros((1, 8 * BLOCK), jnp.float32)
        for n in range(8):
            bias = jnp.where(slot == n, jnp.where(valid[n], 0.0, NEG), bias)
        tiles = tiles_of(fixed, ids)
        scores = dot(ql, tiles, ((1,), (1,))) * SCALE + bias
        top = jnp.max(scores, axis=1, keepdims=True)
        e = jnp.exp(scores - top)
        prob = (e * (1.0 / jnp.sum(e, axis=1, keepdims=True))).astype(jnp.bfloat16)
        pst[zs, b] = prob
        return dot(prob, tiles, ((1,), (0,)))

    def backward(zs, b, ql, gl):
        _, fixed, ids = slots(zs, b)
        tiles = tiles_of(fixed, ids)
        dprob = dot(gl, tiles, ((1,), (1,)))
        low_prob = pst[zs, b]
        prob = low_prob.astype(jnp.float32)
        delta = jnp.sum(prob * dprob, axis=1, keepdims=True)
        dscore = (prob * (dprob - delta) * SCALE).astype(jnp.bfloat16)
        both = jnp.concatenate([low_prob, dscore], axis=0)
        terms = dot(both, jnp.concatenate([gl, ql], axis=0), ((0,), (0,)))
        for n, j in enumerate(fixed):
            acc[j] += terms[n * BLOCK:(n + 1) * BLOCK]
        for n in range(RANDOM):
            trand[zs * 2 * RANDOM + RANDOM * b + n] = terms[(5 + n) * BLOCK:(6 + n) * BLOCK]
        return dot(dscore, tiles, ((1,), (0,)))

    def offset(step):
        odd = step % 2
        return (odd * ((step + 1) // 2) + (1 - odd) * (CHIPS - step // 2)) % CHIPS

    def wide(ref):
        return ref.astype(jnp.float32)

    with jax.named_scope("softmax"):
        @pl.loop(0, CHIPS)
        def _(step):
            off = offset(step)
            zs = behind(off)

            @pl.when(step > 0)
            def _():
                got(qr.at[zs], QS + off)

            qf = qr[zs]
            zero = jnp.zeros_like(qf)
            outs = [softmax(zs, b, jnp.where(low, swap(qf) if b else qf, zero)) for b in range(2)]
            ats[zs] = jnp.where(low, swap(outs[0]), outs[1]).astype(jnp.bfloat16)

            @pl.when(step > 0)
            def _():
                send(ats.at[zs], atr.at[z], AT + off, zdev(zs))

        atr[z] = ats[z]

    def partial_proj():
        with jax.named_scope("attn_back"):
            for off in NEAR:
                got(atr.at[ahead(off)], AT + off)
        with jax.named_scope("partial_proj"):
            attn = jnp.concatenate([
                jnp.concatenate([atr[h][:, :HEAD_DIM] for h in range(HEADS)], axis=1),
                jnp.concatenate([atr[h][:, HEAD_DIM:] for h in range(HEADS)], axis=1)], axis=0)
            for half in range(2):
                f = slice(half * HALF, (half + 1) * HALF)
                pp[half] = dot(attn, go_ref[0, :, f], ((0,), (0,))).astype(jnp.bfloat16)
            send(pp.at[other], pps, RS, sib)

    def proj_x():
        with jax.named_scope("grad_proj_x"):
            got(pps, RS)
            total = wide(pp[c]) + wide(pps[...])
            s1[...] = total.astype(jnp.bfloat16).reshape(ny, nx, 16, HALF)
            for d in range(1, nx):
                xt = (x + d) % nx
                send(s1.at[:, xt], rx.at[d], RX + d, xdev(d))

    def proj_y():
        with jax.named_scope("grad_proj_y"):
            total = wide(s1[:, x])
            for d in range(1, nx):
                got(rx.at[d], RX + d)
                total += wide(rx[d])
            s2[...] = total.astype(jnp.bfloat16)
            for d in range(1, ny):
                send(s2.at[(y + d) % ny], ry.at[d], RY + d, ydev(d))

    def proj_z():
        with jax.named_scope("grad_proj_z"):
            total = wide(s2[y])
            for d in range(1, ny):
                got(ry.at[d], RY + d)
                total += wide(ry[d])
            s3[...] = total.astype(jnp.bfloat16)
            rz[z] = s3[...]
            for off in FAR:
                send(s3, rz.at[z], RZ + off, zdev(ahead(off)))

    def proj_core():
        with jax.named_scope("grad_proj_core"):
            for off in NEAR:
                got(rz.at[behind(off)], RZ + off)
            total = wide(rz[0])
            for k in range(1, CHIPS):
                total += wide(rz[k])
            s4[...] = total
            send(s4, s4b, RF, sib)
            gp_ref[:, mine] = total

    with jax.named_scope("gradients"):
        @pl.loop(0, CHIPS)
        def _(step):
            off = offset(step)
            zs = behind(off)

            @pl.when(step > 0)
            def _():
                got(gr.at[zs], GS + off)

            qf, gf = qr[zs], gr[zs]
            zero = jnp.zeros_like(qf)
            outs = [backward(zs, b, jnp.where(low, swap(qf) if b else qf, zero),
                             jnp.where(low, zero, gf if b else swap(gf))) for b in range(2)]
            dqs[zs] = jnp.where(low, outs[0], swap(outs[1])).astype(jnp.bfloat16)

            @pl.when(step > 0)
            def _():
                send(dqs.at[zs], dqr.at[z], DQ + off, zdev(zs))

            pl.when(step == 3)(partial_proj)
            pl.when(step == 5)(proj_x)

        dqr[z] = dqs[z]

    def pull(o):
        parts = [acc[2 * o], acc[2 * o + 1]]
        for zs in range(CHIPS):
            term = trand[zs * 2 * RANDOM + tbls[zs, 0, o]]
            for w in range(2):
                parts[w] += term * tbls[zs, 0, 16 + 16 * w + o].astype(jnp.float32)
        return parts

    with jax.named_scope("other_core_terms"):
        @pl.loop(0, CHIPS)
        def _(step):
            off = (step + 4) % CHIPS
            k = ahead(off)
            parts = pull(2 * k + other)
            for w in range(2):
                xs[k, w] = parts[w].astype(jnp.bfloat16)
            send(xs.at[k], xr.at[k], XK + off, sib)

    proj_y()

    with jax.named_scope("own_terms"):
        @pl.loop(0, CHIPS)
        def _(step):
            off = (step + 4) % CHIPS
            k = ahead(off)
            parts = pull(2 * k + c)
            got(xr.at[k], XK + off)
            for w in range(2):
                dks[k, w] = (parts[w] + xr[k, w].astype(jnp.float32)).astype(jnp.bfloat16)

            @pl.when(off > 0)
            def _():
                send(dks.at[k], dkr.at[z], DK + off, zdev(k))

        dkr[z] = dks[z]

    proj_z()

    with jax.named_scope("grad_queries"):
        for off in NEAR:
            got(dqr.at[ahead(off)], DQ + off)
        gq_ref[0, :BLOCK] = jnp.concatenate([dqr[h][:, :HEAD_DIM] for h in range(HEADS)], axis=1)
        gq_ref[0, BLOCK:] = jnp.concatenate([dqr[h][:, HEAD_DIM:] for h in range(HEADS)], axis=1)

    proj_core()

    with jax.named_scope("grad_keys_values"):
        for off in NEAR:
            got(dkr.at[behind(off)], DK + off)
        pieces = [dkr[h].reshape(TOKENS, 128) for h in range(HEADS)]
        gk_ref[0] = jnp.concatenate([p[:, :HEAD_DIM] for p in pieces], axis=1)
        gv_ref[0] = jnp.concatenate([p[:, HEAD_DIM:] for p in pieces], axis=1)

    with jax.named_scope("grad_proj_end"):
        got(s4b, RF)
        gp_ref[:, theirs] = s4b[...]

    with jax.named_scope("sent"):
        for d in range(1, ny):
            sent(pj_ref.at[:, mine], PY + d)
            sent(s2.at[(y + d) % ny], RY + d)
        for d in range(1, nx):
            sent(pj.at[c, :, x], PX + d)
            sent(s1.at[:, (x + d) % nx], RX + d)
        sent(pj.at[c], PS)
        sent(pp.at[other], RS)
        sent(s4, RF)
        sent(kvp.at[z], KVF)
        sent(xs.at[z], XK)
        for off in range(1, CHIPS):
            zt, zf = ahead(off), behind(off)
            sent(tblme, TBL + off)
            sent(kvp.at[zt], KV + off)
            sent(kv.at[pl.ds(4 * zf + 2 * c, 2)], KVF + off)
            sent(qp.at[zt], QS + off)
            sent(gpk.at[zt], GS + off)
            sent(ats.at[zf], AT + off)
            sent(dqs.at[zf], DQ + off)
            sent(xs.at[zt], XK + off)
            sent(dks.at[zt], DK + off)
            sent(s3, RZ + off)


def attention_grads(nx, ny, q, k, v, go, rb, proj):
    bf, f32 = jnp.bfloat16, jnp.float32
    rows = nx * ny * 16
    hbm = pl.BlockSpec(memory_space=pl.ANY)
    vmem = pl.BlockSpec(memory_space=pltpu.VMEM)
    scratch = [
        pltpu.VMEM((1, TOKENS, WIDTH), bf),
        pltpu.VMEM((1, TOKENS, WIDTH), bf),
        pltpu.VMEM((1, TOKENS, WIDTH), bf),
        pltpu.VMEM((1, TOKENS, WIDTH), bf),
        pltpu.SMEM((1, 2, RANDOM), jnp.int32),
        pltpu.VMEM((16, WIDTH), bf),
        pltpu.VMEM((8, 128), jnp.int32),
        pltpu.VMEM((CHIPS, 8, 128), jnp.int32),
        pltpu.SMEM((CHIPS, 8, 128), jnp.int32),
        pltpu.VMEM((HEADS, 2, BLOCK, 128), bf),
        pltpu.VMEM((BLOCKS, BLOCK, 128), bf),
        pltpu.VMEM((HEADS, BLOCK, 128), bf),
        pltpu.VMEM((CHIPS, BLOCK, 128), bf),
        pltpu.VMEM((HEADS, BLOCK, 128), bf),
        pltpu.VMEM((CHIPS, BLOCK, 128), bf),
        pltpu.VMEM((2, ny, nx, 16, HALF), bf),
        pltpu.VMEM((CHIPS, 2, BLOCK, 8 * BLOCK), bf),
        pltpu.VMEM((BLOCKS, BLOCK, 128), f32),
        pltpu.VMEM((CHIPS * 2 * RANDOM, BLOCK, 128), f32),
        pltpu.VMEM((CHIPS, BLOCK, 128), bf),
        pltpu.VMEM((HEADS, BLOCK, 128), bf),
        pltpu.VMEM((CHIPS, BLOCK, 128), bf),
        pltpu.VMEM((HEADS, BLOCK, 128), bf),
        pltpu.VMEM((CHIPS, 2, BLOCK, 128), bf),
        pltpu.VMEM((CHIPS, 2, BLOCK, 128), bf),
        pltpu.VMEM((CHIPS, 2, BLOCK, 128), bf),
        pltpu.VMEM((HEADS, 2, BLOCK, 128), bf),
        pltpu.VMEM((2, rows, HALF), bf),
        pltpu.VMEM((rows, HALF), bf),
        pltpu.VMEM((ny, nx, 16, HALF), bf),
        pltpu.VMEM((nx, ny, 16, HALF), bf),
        pltpu.VMEM((ny, 16, HALF), bf),
        pltpu.VMEM((ny, 16, HALF), bf),
        pltpu.VMEM((16, HALF), bf),
        pltpu.VMEM((CHIPS, 16, HALF), bf),
        pltpu.VMEM((16, HALF), f32),
        pltpu.VMEM((16, HALF), f32),
        pltpu.SemaphoreType.DMA((SEMS,)),
        pltpu.SemaphoreType.DMA((SEMS,)),
        pltpu.SemaphoreType.DMA((7,)),
    ]
    tokens = jax.ShapeDtypeStruct((1, TOKENS, WIDTH), bf)
    return pl.pallas_call(
        functools.partial(kernel, nx, ny),
        out_shape=[tokens, tokens, tokens, jax.ShapeDtypeStruct((16, WIDTH), f32)],
        in_specs=[hbm] * 6,
        out_specs=[vmem, vmem, vmem, vmem],
        scratch_shapes=scratch,
        compiler_params=pltpu.CompilerParams(
            collective_id=0, has_side_effects=True, vmem_limit_bytes=48 * 1024 * 1024),
        cost_estimate=pl.CostEstimate(
            flops=2 * 500_000_000, bytes_accessed=2_000_000, transcendentals=600_000),
    )(q, k, v, go, rb, proj)


def solution(mesh, nx=4, ny=8):
    tokens = P("dp", "seq", None)
    return jax.shard_map(
        functools.partial(attention_grads, nx, ny),
        mesh=mesh,
        in_specs=(tokens, tokens, tokens, tokens, tokens, P("dp", None)),
        out_specs=(tokens, tokens, tokens, P("dp", None)),
        check_vma=False,
    )
```

time: 77.7 us -> 68.6 us (0.88)
  Pallas kernels: 69.2 us -> 60.1 us
    pallas_call x1, Pallas kernels: 69.2 us -> 60.1 us  [attention_grads(): pl.pallas_call(functools.partial(kernel, nx, ny), out_shape=[tokens, toke...]
where the time goes in v2:
time: 68.6 us; the launch traced here: 68.3 us
  Pallas kernels  60.1 us (88%)
  local copies, waits for them, and re-layouts  7.59 us (11%)
    pallas_call x1, Pallas kernels, attention_grads(): pl.pallas_call(functools.partial(kernel, nx, ny), out_shape=[tokens, toke...  60.1 us
    unnamed x16, local copies, waits for them, and re-layouts  7.59 us

profile of v2, /device:TPU:1, one launch (start us, length us, event | category | flops | bytes accessed | tf_op | source)
XLA Modules:
  0.0 68.3 jit_solution(6433179385244726255)
XLA Ops:
  0.6 0.0 copy-start
  0.6 0.9 %copy-done = bf16[1,128,512]{2,1,0:T(8,128)(2,1)S(1)} copy-done((bf16[1,128,512]{2,1,0:T(8,128)(2,1)S(1)}, bf16[1,128,512]{2,1,0:T(8,128)(2,1)}, u32[]{:S(2)}) %copy-start) | copy-done | bytes 131096
  1.5 0.0 copy-start.1
  1.5 0.9 %copy-done.1 = bf16[1,128,512]{2,1,0:T(8,128)(2,1)S(1)} copy-done((bf16[1,128,512]{2,1,0:T(8,128)(2,1)S(1)}, bf16[1,128,512]{2,1,0:T(8,128)(2,1)}, u32[]{:S(2)}) %copy-start.1) | copy-done | bytes 131096
  2.4 0.0 copy-start.2
  2.4 0.9 %copy-done.2 = bf16[1,128,512]{2,1,0:T(8,128)(2,1)S(1)} copy-done((bf16[1,128,512]{2,1,0:T(8,128)(2,1)S(1)}, bf16[1,128,512]{2,1,0:T(8,128)(2,1)}, u32[]{:S(2)}) %copy-start.2) | copy-done | bytes 131096
  3.3 0.0 copy-start.3
  3.3 0.9 %copy-done.3 = bf16[1,128,512]{2,1,0:T(8,128)(2,1)S(1)} copy-done((bf16[1,128,512]{2,1,0:T(8,128)(2,1)S(1)}, bf16[1,128,512]{2,1,0:T(8,128)(2,1)}, u32[]{:S(2)}) %copy-start.3) | copy-done | bytes 131096
  4.3 0.0 copy-start.4
  4.3 0.7 %copy-done.4 = bf16[16,512]{1,0:T(8,128)(2,1)S(1)} copy-done((bf16[16,512]{1,0:T(8,128)(2,1)S(1)}, bf16[16,512]{1,0:T(8,128)(2,1)}, u32[]{:S(2)}) %copy-start.4) | copy-done | bytes 16408
  5.0 0.0 copy-start.5
  5.0 0.7 copy-done.5
  5.6 60.1 %shard_map.93 = (bf16[1,128,512]{2,1,0:T(8,128)(2,1)S(1)}, bf16[1,128,512]{2,1,0:T(8,128)(2,1)S(1)}, bf16[1,128,512]{2,1,0:T(8,128)(2,1)S(1)}, f32[16,512]{1,0:T(8,128)S(1)}) custom-call(bf16[1,128,512]{2,1,0:T(8,128)(2,1)S(1)} %copy-done, bf16[1,128,512]{2,1,0:T(8,128)(2,1)S(1)} %copy-done.1, bf16[1,128,512]{2,1,0:T(8,128)(2,1)S(1)} %copy-done.2, ...), custom_call_target="tpu_custom_call" | custom-call | flops 1000000000 | bytes 2000000 | tf_op jit(solution)/shard_map/pallas_call | solution.py:477
  65.7 0.7 copy.14
  66.4 0.7 copy.15
  67.1 0.7 copy.16
  67.7 0.6 copy.17
Async XLA Ops:
  0.6 0.9 %copy-start = (bf16[1,128,512]{2,1,0:T(8,128)(2,1)S(1)}, bf16[1,128,512]{2,1,0:T(8,128)(2,1)}, u32[]{:S(2)}) copy-start(bf16[1,128,512]{2,1,0:T(8,128)(2,1)} %q_hbm.1) | copy-start | bytes 393220
  1.5 0.9 %copy-start.1 = (bf16[1,128,512]{2,1,0:T(8,128)(2,1)S(1)}, bf16[1,128,512]{2,1,0:T(8,128)(2,1)}, u32[]{:S(2)}) copy-start(bf16[1,128,512]{2,1,0:T(8,128)(2,1)} %k_hbm.1) | copy-start | bytes 393220
  2.4 0.9 %copy-start.2 = (bf16[1,128,512]{2,1,0:T(8,128)(2,1)S(1)}, bf16[1,128,512]{2,1,0:T(8,128)(2,1)}, u32[]{:S(2)}) copy-start(bf16[1,128,512]{2,1,0:T(8,128)(2,1)} %v_hbm.1) | copy-start | bytes 393220
  3.3 0.9 %copy-start.3 = (bf16[1,128,512]{2,1,0:T(8,128)(2,1)S(1)}, bf16[1,128,512]{2,1,0:T(8,128)(2,1)}, u32[]{:S(2)}) copy-start(bf16[1,128,512]{2,1,0:T(8,128)(2,1)} %go_hbm.1) | copy-start | bytes 393220
  4.3 0.7 %copy-start.4 = (bf16[16,512]{1,0:T(8,128)(2,1)S(1)}, bf16[16,512]{1,0:T(8,128)(2,1)}, u32[]{:S(2)}) copy-start(bf16[16,512]{1,0:T(8,128)(2,1)} %pj_hbm.1) | copy-start | bytes 49156
  5.0 0.7 copy-start.5

commit v3 on v2

v3 whole, which is shorter than its diff:
```python
import functools

import jax
import jax.numpy as jnp
from jax import lax
from jax.experimental import pallas as pl
from jax.experimental.pallas import tpu as pltpu
from jax.sharding import PartitionSpec as P

HEADS = 8
HEAD_DIM = 64
BLOCK = 64
RANDOM = 3
CHIPS = 8
TOKENS = 128
WIDTH = 512
HALF = 256
BLOCKS = 32
SCALE = HEAD_DIM ** (-0.5)
NEG = -1e30
NEAR = (1, 7, 2, 6, 3, 5, 4)
FAR = (4, 3, 5, 2, 6, 1, 7)
PER = 2
VMEM = 40 * 1024 * 1024

KVF, QS, GS, TBL, PY, PX, PS, AT, DQ, XK, DK, RS, RX, RY, RZ, RF = range(16)
KV, XKR, SEMS = 16, 24, 32
EXP2 = SCALE * 1.4426950408889634


def dot(a, b, dims):
    return lax.dot_general(a, b, (dims, ((), ())), preferred_element_type=jnp.float32)


def halves(a, b):
    return jnp.concatenate([a, b], axis=1)


def kernel(nx, ny, q_hbm, k_hbm, v_hbm, go_hbm, rb_hbm, pj_hbm, gq_ref, gk_ref, gv_ref, gp_ref,
           q_ref, k_ref, v_ref, go_ref, rb_ref, pj_ref,
           tblme, tblv, tbls, kvp, kv, kk, vv, qp, qr, gpk, gr, pj, pst, acc, trand, ats, atr, dqs, dqr,
           xs, xr, dks, dkr, pp, pps, s1, rx, s2, ry, s3, rz, s4, s4b, ssem, rsem, lsem):
    dp = lax.axis_index("dp")
    s = lax.axis_index("seq")
    z, c = s // 2, s % 2
    y, x = dp // nx, dp % nx
    other = 1 - c
    sib = (dp, 2 * z + other)

    def zdev(zt):
        return (dp, 2 * zt + c)

    def xdev(d):
        return (y * nx + (x + d) % nx, s)

    def ydev(d):
        return (((y + d) % ny) * nx + x, s)

    def send(src, dst, sem, dev, arrival=None):
        arrival = sem if arrival is None else arrival
        copy = pltpu.make_async_remote_copy(
            src_ref=src, dst_ref=dst, send_sem=ssem.at[sem], recv_sem=rsem.at[arrival],
            device_id=dev, device_id_type=pl.DeviceIdType.MESH)
        copy.start()

    def got(dst, sem):
        pltpu.make_async_remote_copy(
            src_ref=dst, dst_ref=dst, send_sem=ssem.at[0], recv_sem=rsem.at[sem],
            device_id=sib, device_id_type=pl.DeviceIdType.MESH).wait_recv()

    def sent(src, sem):
        pltpu.make_async_remote_copy(
            src_ref=src, dst_ref=src, send_sem=ssem.at[sem], recv_sem=rsem.at[0],
            device_id=sib, device_id_type=pl.DeviceIdType.MESH).wait_send()

    def ahead(off):
        return (z + off) % CHIPS

    def behind(off):
        return (z + CHIPS - off) % CHIPS

    barrier = pltpu.get_barrier_semaphore()
    partners = [sib] + [zdev(ahead(off)) for off in range(1, CHIPS)]
    partners += [xdev(d) for d in range(1, nx)] + [ydev(d) for d in range(1, ny)]
    for dev in partners:
        pl.semaphore_signal(barrier, inc=1, device_id=dev, device_id_type=pl.DeviceIdType.MESH)

    loads = [pltpu.make_async_copy(a, b, lsem.at[1 + n]) for n, (a, b) in enumerate((
        (pj_hbm, pj_ref), (rb_hbm, rb_ref), (k_hbm, k_ref), (v_hbm, v_ref), (q_hbm, q_ref),
        (go_hbm, go_ref)))]
    for load in loads:
        load.start()

    mine = pl.ds(pl.multiple_of(c * HALF, HALF), HALF)
    theirs = pl.ds(pl.multiple_of(other * HALF, HALF), HALF)

    low = lax.broadcasted_iota(jnp.int32, (BLOCK, 128), 1) < HEAD_DIM

    def swap(a):
        return halves(a[:, HEAD_DIM:], a[:, :HEAD_DIM])

    def fill(source):
        for n in range(2):
            j = 2 * source + n
            pair = kv[j]
            turned = swap(pair)
            kk[j] = jnp.where(low, pair, turned)
            vv[j] = jnp.where(low, turned, pair)

    with jax.named_scope("pack_inputs"):
        loads[0].wait()
        loads[1].wait()
        pj[c, y, x] = pj_ref[:, mine]
        lane = lax.broadcasted_iota(jnp.int32, (8, 128), 1)
        row = jnp.zeros((8, 128), jnp.int32)
        for e in range(2 * RANDOM):
            block = rb_ref[0, e // RANDOM, e % RANDOM]
            own = block // 2
            row = jnp.where(lane == own, e, row)
            row = jnp.where(lane == own + 16 + 16 * (block % 2), 1, row)
            row = jnp.where(lane == 48 + e, block, row)
        tblme[...] = row
        tblv[z] = row
        loads[2].wait()
        loads[3].wait()
        for h in range(HEADS):
            f = slice(h * HEAD_DIM, (h + 1) * HEAD_DIM)
            kvp[h] = halves(k_ref[0, :, f], v_ref[0, :, f]).reshape(2, BLOCK, 128)
        kv[pl.ds(2 * s, 2)] = kvp[z]
        loads[4].wait()
        for h in range(HEADS):
            f = slice(h * HEAD_DIM, (h + 1) * HEAD_DIM)
            qp[h] = halves(q_ref[0, :BLOCK, f], q_ref[0, BLOCK:, f])
        qr[z] = qp[z]
        fill(s)

    with jax.named_scope("barrier"):
        pl.semaphore_wait(barrier, len(partners))

    with jax.named_scope("first_sends"):
        for d in range(1, ny):
            send(pj_ref.at[:, mine], pj.at[c, y, x], PY, ydev(d))
        for off in FAR:
            zt = ahead(off)
            send(kvp.at[zt], kv.at[pl.ds(2 * s, 2)], KV, zdev(zt), KV + off)
        send(kvp.at[z], kv.at[pl.ds(2 * s, 2)], KVF, sib)
        for off in FAR:
            send(tblme, tblv.at[z], TBL, zdev(ahead(off)))
        for off in FAR:
            zt = ahead(off)
            send(qp.at[zt], qr.at[z], QS, zdev(zt))

    acc[...] = jnp.zeros_like(acc)

    with jax.named_scope("proj_rows_y"):
        got(pj.at[c, pl.ds(0, ny - 1), 0], PY)
        for d in range(1, nx):
            send(pj.at[c, :, x], pj.at[c, :, x], PX, xdev(d))

    def forward(off):
        zf = behind(off)
        part = kv.at[pl.ds(4 * zf + 2 * c, 2)]
        got(part, KV + off)
        send(part, part, KVF, sib)
        fill(2 * zf + c)

    with jax.named_scope("forward_a"):
        for off in NEAR[:4]:
            forward(off)

    with jax.named_scope("proj_rows_x"):
        got(pj.at[c, :, pl.ds(0, nx - 1)], PX)
        send(pj.at[c], pj.at[c], PS, sib)

    with jax.named_scope("forward_b"):
        for off in NEAR[4:]:
            forward(off)

    with jax.named_scope("tables"):
        got(tblv.at[pl.ds(0, CHIPS - 1)], TBL)
        table = pltpu.make_async_copy(tblv, tbls, lsem.at[0])
        table.start()
    with jax.named_scope("proj_other"):
        got(pj.at[other], PS)
        loads[5].wait()
    with jax.named_scope("grad_attn"):
        rows = nx * ny * 16
        ga = dot(go_ref[0, :, :HALF], pj[0].reshape(rows, HALF), ((1,), (1,)))
        ga += dot(go_ref[0, :, HALF:], pj[1].reshape(rows, HALF), ((1,), (1,)))
        ga = ga.astype(jnp.bfloat16)
        for h in range(HEADS):
            f = slice(h * HEAD_DIM, (h + 1) * HEAD_DIM)
            gpk[h] = halves(ga[:BLOCK, f], ga[BLOCK:, f])
        gr[z] = gpk[z]
        for off in FAR:
            zt = ahead(off)
            send(gpk.at[zt], gr.at[z], GS, zdev(zt))

    with jax.named_scope("other_core_keys"):
        table.wait()
        got(kv.at[pl.ds(0, 2 * CHIPS)], KVF)
        for k in range(CHIPS):
            fill(2 * k + other)

    high = jnp.logical_not(low)
    none = jnp.zeros((BLOCK, 128), jnp.bfloat16)

    def diagonal(a, b):
        return jnp.concatenate([jnp.where(low, a, none), jnp.where(high, b, none)], axis=0)

    def slots(zs, b):
        i = 4 * zs + 2 * c + b
        fixed = (jnp.maximum(i - 1, 0), i, jnp.minimum(i + 1, BLOCKS - 1), 0, 1)
        return i, fixed, [tbls[zs, 0, 48 + RANDOM * b + n] for n in range(RANDOM)]

    def paired(ref, blocks):
        return jnp.concatenate(
            [jnp.where(low, ref[a], ref[b]) for a, b in zip(*blocks)], axis=0)

    def named(zs):
        return [list(fixed) + ids for _, fixed, ids in (slots(zs, b) for b in range(2))]

    def softmax(zs):
        biases = []
        for b in range(2):
            i, fixed, ids = slots(zs, b)
            valid = [i >= 1, i >= 0, i < BLOCKS - 1, i >= 2, i >= 3]
            for n in range(RANDOM):
                r = ids[n]
                clash = (r == i - 1) | (r == i) | (r == i + 1) | (r <= 1)
                for earlier in ids[:n]:
                    clash = clash | (r == earlier)
                valid.append(jnp.logical_not(clash))
            biases.append([jnp.where(v, 0.0, NEG) for v in valid])
        qf = qr[zs]
        blocks = named(zs)
        scores = dot(paired(kk, blocks), diagonal(qf, qf), ((1,), (1,)))
        scores = jnp.concatenate([
            scores[n * BLOCK:(n + 1) * BLOCK] + jnp.where(low[:1], biases[0][n], biases[1][n])
            for n in range(8)], axis=0)
        top = jnp.max(scores, axis=0, keepdims=True)
        e = jnp.exp2((scores - top) * EXP2)
        prob = (e * (1.0 / jnp.sum(e, axis=0, keepdims=True))).astype(jnp.bfloat16)
        pst[zs] = prob
        out = dot(prob, paired(vv, blocks), ((0,), (0,)))
        ats[zs] = jnp.where(low, out[:BLOCK], out[BLOCK:]).astype(jnp.bfloat16)

    def backward(zs):
        qf, gf = qr[zs], gr[zs]
        blocks = named(zs)
        dprob = dot(paired(vv, blocks), diagonal(gf, gf) * SCALE, ((1,), (1,)))
        low_prob = pst[zs]
        prob = low_prob.astype(jnp.float32)
        delta = jnp.sum(prob * dprob, axis=0, keepdims=True)
        dscore = (prob * (dprob - delta)).astype(jnp.bfloat16)
        out = dot(dscore, paired(kk, blocks), ((0,), (0,)))
        dqs[zs] = jnp.where(low, out[:BLOCK], out[BLOCK:]).astype(jnp.bfloat16)
        wide_low = jnp.concatenate([low] * 8, axis=0)
        sides = (jnp.where(wide_low, dscore, swap(low_prob)),
                 jnp.where(wide_low, swap(dscore), low_prob))
        right = (diagonal(qf, swap(gf)), diagonal(swap(qf), gf))
        terms = [dot(sides[b], right[b], ((1,), (0,))) for b in range(2)]
        return blocks, terms

    def collect(zs, blocks, terms):
        for b in range(2):
            for n in range(5):
                acc[blocks[b][n]] += terms[b][n * BLOCK:(n + 1) * BLOCK]
            for n in range(RANDOM):
                trand[zs * 2 * RANDOM + RANDOM * b + n] = terms[b][(5 + n) * BLOCK:(6 + n) * BLOCK]

    def far(step, n):
        k = step * (PER // 2) + n // 2
        return ahead(CHIPS // 2 - k if n % 2 else (CHIPS // 2 + 1 + k) % CHIPS)

    def wide(ref):
        return ref.astype(jnp.float32)

    with jax.named_scope("queries_wait"):
        got(qr.at[pl.ds(0, CHIPS - 1)], QS)
    with jax.named_scope("softmax"):
        @pl.loop(0, CHIPS // PER)
        def _(step):
            sources = [far(step, n) for n in range(PER)]
            for zs in sources:
                softmax(zs)
            for n, zs in enumerate(sources):
                if n < PER - 2:
                    send(ats.at[zs], atr.at[z], AT, zdev(zs))
                elif n == PER - 1:
                    send(ats.at[zs], atr.at[z], AT, zdev(zs))
                else:
                    @pl.when(step < CHIPS // PER - 1)
                    def _():
                        send(ats.at[zs], atr.at[z], AT, zdev(zs))

        atr[z] = ats[z]

    def partial_proj():
        with jax.named_scope("attn_back"):
            got(atr.at[pl.ds(0, CHIPS - 1)], AT)
        with jax.named_scope("partial_proj"):
            attn = jnp.concatenate([
                jnp.concatenate([atr[h][:, :HEAD_DIM] for h in range(HEADS)], axis=1),
                jnp.concatenate([atr[h][:, HEAD_DIM:] for h in range(HEADS)], axis=1)], axis=0)
            for half in range(2):
                f = slice(half * HALF, (half + 1) * HALF)
                pp[half] = dot(attn, go_ref[0, :, f], ((0,), (0,))).astype(jnp.bfloat16)
            send(pp.at[other], pps, RS, sib)

    def proj_x():
        with jax.named_scope("grad_proj_x"):
            got(pps, RS)
            total = wide(pp[c]) + wide(pps[...])
            s1[...] = total.astype(jnp.bfloat16).reshape(ny, nx, 16, HALF)
            for d in range(1, nx):
                xt = (x + d) % nx
                send(s1.at[:, xt], rx.at[d], RX, xdev(d))

    def proj_y():
        with jax.named_scope("grad_proj_y"):
            total = wide(s1[:, x])
            got(rx.at[pl.ds(1, nx - 1)], RX)
            for d in range(1, nx):
                total += wide(rx[d])
            s2[...] = total.astype(jnp.bfloat16)
            for d in range(1, ny):
                send(s2.at[(y + d) % ny], ry.at[d], RY, ydev(d))

    def proj_z():
        with jax.named_scope("grad_proj_z"):
            total = wide(s2[y])
            got(ry.at[pl.ds(1, ny - 1)], RY)
            for d in range(1, ny):
                total += wide(ry[d])
            s3[...] = total.astype(jnp.bfloat16)
            rz[z] = s3[...]
            for off in FAR:
                send(s3, rz.at[z], RZ, zdev(ahead(off)))

    def proj_core():
        with jax.named_scope("grad_proj_core"):
            got(rz.at[pl.ds(0, CHIPS - 1)], RZ)
            total = wide(rz[0])
            for k in range(1, CHIPS):
                total += wide(rz[k])
            s4[...] = total
            send(s4, s4b, RF, sib)
            gp_ref[:, mine] = total

    with jax.named_scope("grad_attn_wait"):
        got(gr.at[pl.ds(0, CHIPS - 1)], GS)
    with jax.named_scope("gradients"):
        @pl.loop(0, CHIPS // PER)
        def _(step):
            sources = [far(step, n) for n in range(PER)]
            results = [backward(zs) for zs in sources]
            for zs, (blocks, terms) in zip(sources, results):
                collect(zs, blocks, terms)
            for n, zs in enumerate(sources):
                if n < PER - 2:
                    send(dqs.at[zs], dqr.at[z], DQ, zdev(zs))
                elif n == PER - 1:
                    send(dqs.at[zs], dqr.at[z], DQ, zdev(zs))
                else:
                    @pl.when(step < CHIPS // PER - 1)
                    def _():
                        send(dqs.at[zs], dqr.at[z], DQ, zdev(zs))

            pl.when(step == 0)(partial_proj)
            pl.when(step == 1)(proj_x)

        dqr[z] = dqs[z]

    def pull(o):
        parts = [acc[2 * o], acc[2 * o + 1]]
        for zs in range(CHIPS):
            term = trand[zs * 2 * RANDOM + tbls[zs, 0, o]]
            for w in range(2):
                parts[w] += term * tbls[zs, 0, 16 + 16 * w + o].astype(jnp.float32)
        return parts

    with jax.named_scope("other_core_terms"):
        @pl.loop(0, CHIPS)
        def _(step):
            off = (step + 4) % CHIPS
            k = ahead(off)
            parts = pull(2 * k + other)
            for w in range(2):
                xs[k, w] = parts[w].astype(jnp.bfloat16)
            send(xs.at[k], xr.at[k], XK, sib, XKR + off)

    with jax.named_scope("own_terms"):
        @pl.loop(0, CHIPS)
        def _(step):
            off = (step + 4) % CHIPS
            k = ahead(off)
            parts = pull(2 * k + c)
            got(xr.at[k], XKR + off)
            for w in range(2):
                dks[k, w] = (parts[w] + xr[k, w].astype(jnp.float32)).astype(jnp.bfloat16)

            @pl.when(off > 0)
            def _():
                send(dks.at[k], dkr.at[z], DK, zdev(k))

        dkr[z] = dks[z]

    proj_y()
    proj_z()

    with jax.named_scope("grad_queries"):
        got(dqr.at[pl.ds(0, CHIPS - 1)], DQ)
        gq_ref[0, :BLOCK] = jnp.concatenate([dqr[h][:, :HEAD_DIM] for h in range(HEADS)], axis=1)
        gq_ref[0, BLOCK:] = jnp.concatenate([dqr[h][:, HEAD_DIM:] for h in range(HEADS)], axis=1)

    proj_core()

    with jax.named_scope("grad_keys_values"):
        got(dkr.at[pl.ds(0, CHIPS - 1)], DK)
        pieces = [dkr[h].reshape(TOKENS, 128) for h in range(HEADS)]
        gk_ref[0] = jnp.concatenate([p[:, :HEAD_DIM] for p in pieces], axis=1)
        gv_ref[0] = jnp.concatenate([p[:, HEAD_DIM:] for p in pieces], axis=1)

    with jax.named_scope("grad_proj_end"):
        got(s4b, RF)
        gp_ref[:, theirs] = s4b[...]

    with jax.named_scope("sent"):
        rest = pl.ds(0, CHIPS - 1)
        sent(pj.at[0, pl.ds(0, ny - 1), 0], PY)
        sent(pj.at[0, :, pl.ds(0, nx - 1)], PX)
        sent(pj.at[0], PS)
        sent(tblv.at[rest], TBL)
        sent(kvp.at[rest], KV)
        sent(kvp, KVF)
        sent(qp.at[rest], QS)
        sent(gpk.at[rest], GS)
        sent(ats.at[rest], AT)
        sent(dqs.at[rest], DQ)
        sent(xs, XK)
        sent(dks.at[rest], DK)
        sent(pps, RS)
        sent(s1.at[:, pl.ds(0, nx - 1)], RX)
        sent(s2.at[pl.ds(0, ny - 1)], RY)
        sent(rz.at[rest], RZ)
        sent(s4, RF)


def store(*refs):
    count = len(refs) // 2
    copies = [pltpu.make_async_copy(refs[n], refs[count + n], refs[-1].at[n]) for n in range(count)]
    for copy in copies:
        copy.start()
    for copy in copies:
        copy.wait()


def attention_grads(nx, ny, q, k, v, go, rb, proj):
    bf, f32 = jnp.bfloat16, jnp.float32
    rows = nx * ny * 16
    hbm = pl.BlockSpec(memory_space=pltpu.HBM)
    vmem = pl.BlockSpec(memory_space=pltpu.VMEM)
    scratch = [
        pltpu.VMEM((1, TOKENS, WIDTH), bf),
        pltpu.VMEM((1, TOKENS, WIDTH), bf),
        pltpu.VMEM((1, TOKENS, WIDTH), bf),
        pltpu.VMEM((1, TOKENS, WIDTH), bf),
        pltpu.SMEM((1, 2, RANDOM), jnp.int32),
        pltpu.VMEM((16, WIDTH), bf),
        pltpu.VMEM((8, 128), jnp.int32),
        pltpu.VMEM((CHIPS, 8, 128), jnp.int32),
        pltpu.SMEM((CHIPS, 8, 128), jnp.int32),
        pltpu.VMEM((HEADS, 2, BLOCK, 128), bf),
        pltpu.VMEM((BLOCKS, BLOCK, 128), bf),
        pltpu.VMEM((BLOCKS, BLOCK, 128), bf),
        pltpu.VMEM((BLOCKS, BLOCK, 128), bf),
        pltpu.VMEM((HEADS, BLOCK, 128), bf),
        pltpu.VMEM((CHIPS, BLOCK, 128), bf),
        pltpu.VMEM((HEADS, BLOCK, 128), bf),
        pltpu.VMEM((CHIPS, BLOCK, 128), bf),
        pltpu.VMEM((2, ny, nx, 16, HALF), bf),
        pltpu.VMEM((CHIPS, 8 * BLOCK, 128), bf),
        pltpu.VMEM((BLOCKS, BLOCK, 128), f32),
        pltpu.VMEM((CHIPS * 2 * RANDOM, BLOCK, 128), f32),
        pltpu.VMEM((CHIPS, BLOCK, 128), bf),
        pltpu.VMEM((HEADS, BLOCK, 128), bf),
        pltpu.VMEM((CHIPS, BLOCK, 128), bf),
        pltpu.VMEM((HEADS, BLOCK, 128), bf),
        pltpu.VMEM((CHIPS, 2, BLOCK, 128), bf),
        pltpu.VMEM((CHIPS, 2, BLOCK, 128), bf),
        pltpu.VMEM((CHIPS, 2, BLOCK, 128), bf),
        pltpu.VMEM((HEADS, 2, BLOCK, 128), bf),
        pltpu.VMEM((2, rows, HALF), bf),
        pltpu.VMEM((rows, HALF), bf),
        pltpu.VMEM((ny, nx, 16, HALF), bf),
        pltpu.VMEM((nx, ny, 16, HALF), bf),
        pltpu.VMEM((ny, 16, HALF), bf),
        pltpu.VMEM((ny, 16, HALF), bf),
        pltpu.VMEM((16, HALF), bf),
        pltpu.VMEM((CHIPS, 16, HALF), bf),
        pltpu.VMEM((16, HALF), f32),
        pltpu.VMEM((16, HALF), f32),
        pltpu.SemaphoreType.DMA((SEMS,)),
        pltpu.SemaphoreType.DMA((SEMS,)),
        pltpu.SemaphoreType.DMA((7,)),
    ]
    tokens = jax.ShapeDtypeStruct((1, TOKENS, WIDTH), bf)
    shapes = [tokens, tokens, tokens, jax.ShapeDtypeStruct((16, WIDTH), f32)]
    grads = pl.pallas_call(
        functools.partial(kernel, nx, ny),
        out_shape=shapes,
        in_specs=[hbm] * 6,
        out_specs=[vmem, vmem, vmem, vmem],
        scratch_shapes=scratch,
        compiler_params=pltpu.CompilerParams(
            collective_id=0, has_side_effects=True, vmem_limit_bytes=VMEM),
        cost_estimate=pl.CostEstimate(
            flops=2 * 500_000_000, bytes_accessed=2_000_000, transcendentals=600_000),
    )(*[pltpu.with_memory_space_constraint(a, pltpu.HBM) for a in (q, k, v, go, rb, proj)])
    return pl.pallas_call(
        store,
        out_shape=shapes,
        in_specs=[vmem] * 4,
        out_specs=[hbm] * 4,
        scratch_shapes=[pltpu.SemaphoreType.DMA((4,))],
        compiler_params=pltpu.CompilerParams(vmem_limit_bytes=1024 * 1024),
    )(*grads)


def solution(mesh, nx=4, ny=8):
    tokens = P("dp", "seq", None)
    return jax.shard_map(
        functools.partial(attention_grads, nx, ny),
        mesh=mesh,
        in_specs=(tokens, tokens, tokens, tokens, tokens, P("dp", None)),
        out_specs=(tokens, tokens, tokens, P("dp", None)),
        check_vma=False,
    )
```

time: 68.6 us -> 55.2 us (0.80)
  local copies, waits for them, and re-layouts: 7.59 us -> 0 us
  Pallas kernels: 60.1 us -> 54.4 us
    unnamed x16 -> x0, local copies, waits for them, and re-layouts: 7.59 us -> none
    pallas_call x1 -> x2, Pallas kernels: 60.1 us -> 54.4 us  [the longest x1 53.6 us: attention_grads(): pl.pallas_call(functools.partial(kernel, nx, ny), out_shape=shapes, in_sp...]
where the time goes in v3:
time: 55.2 us; the launch traced here: 55 us
  Pallas kernels  54.4 us (99%)
  between operations  0.64 us (1%)
    pallas_call x1, Pallas kernels, attention_grads(): pl.pallas_call(functools.partial(kernel, nx, ny), out_shape=shapes, in_sp...  53.6 us

profile of v3, /device:TPU:1, one launch (start us, length us, event | category | flops | bytes accessed | tf_op | source)
XLA Modules:
  0.0 55.0 jit_solution(16941901193994830414)
XLA Ops:
  0.6 53.6 %shard_map.93 = (bf16[1,128,512]{2,1,0:T(8,128)(2,1)S(1)}, bf16[1,128,512]{2,1,0:T(8,128)(2,1)S(1)}, bf16[1,128,512]{2,1,0:T(8,128)(2,1)S(1)}, f32[16,512]{1,0:T(8,128)S(1)}) custom-call(bf16[1,128,512]{2,1,0:T(8,128)(2,1)} %q_hbm.1, bf16[1,128,512]{2,1,0:T(8,128)(2,1)} %k_hbm.1, bf16[1,128,512]{2,1,0:T(8,128)(2,1)} %v_hbm.1, bf16[1,128,512]{2,1,0:T(8,128)(2,1)} %go_hbm.1, ...), custom_call_target="tpu_custom_call" | custom-call | flops 1000000000 | bytes 2000000 | tf_op jit(solution)/shard_map/pallas_call | solution.py:510
  54.2 0.8 %shard_map.94 = (bf16[1,128,512]{2,1,0:T(8,128)(2,1)}, bf16[1,128,512]{2,1,0:T(8,128)(2,1)}, bf16[1,128,512]{2,1,0:T(8,128)(2,1)}, f32[16,512]{1,0:T(8,128)}) custom-call(bf16[1,128,512]{2,1,0:T(8,128)(2,1)S(1)} %get-tuple-element.8.refs_0_, bf16[1,128,512]{2,1,0:T(8,128)(2,1)S(1)} %get-tuple-element.9.refs_1_, ...), custom_call_target="tpu_custom_call" | custom-call | tf_op jit(solution)/shard_map/pallas_call | solution.py:521

commit v4 on v3

--- a/solution.py
+++ b/solution.py
@@ -18,12 +18,11 @@
 BLOCKS = 32
 SCALE = HEAD_DIM ** (-0.5)
 NEG = -1e30
-NEAR = (1, 7, 2, 6, 3, 5, 4)
 FAR = (4, 3, 5, 2, 6, 1, 7)
-PER = 2
+PART = 4
 VMEM = 40 * 1024 * 1024
 
-KVF, QS, GS, TBL, PY, PX, PS, AT, DQ, XK, DK, RS, RX, RY, RZ, RF = range(16)
+KVF, QS, GS, TBL, PY, PX, PS, AT, DQ, XK, DK, RS, RX, RZ = range(14)
 KV, XKR, SEMS = 16, 24, 32
 EXP2 = SCALE * 1.4426950408889634
 
@@ -38,8 +37,8 @@
 
 def kernel(nx, ny, q_hbm, k_hbm, v_hbm, go_hbm, rb_hbm, pj_hbm, gq_ref, gk_ref, gv_ref, gp_ref,
            q_ref, k_ref, v_ref, go_ref, rb_ref, pj_ref,
-           tblme, tblv, tbls, kvp, kv, kk, vv, qp, qr, gpk, gr, pj, pst, acc, trand, ats, atr, dqs, dqr,
-           xs, xr, dks, dkr, pp, pps, s1, rx, s2, ry, s3, rz, s4, s4b, ssem, rsem, lsem):
+           tblme, tblv, tbls, kvp, kv, kk, vv, qp, qr, gpk, gr, pj, sst, pst, dst, acc, trand, ats, atr, dqs, dqr,
+           xs, xr, dks, dkr, pp, pps, s1, rx, s3, rz, ssem, rsem, lsem):
     dp = lax.axis_index("dp")
     s = lax.axis_index("seq")
     z, c = s // 2, s % 2
@@ -80,8 +79,9 @@
         return (z + CHIPS - off) % CHIPS
 
     barrier = pltpu.get_barrier_semaphore()
-    partners = [sib] + [zdev(ahead(off)) for off in range(1, CHIPS)]
-    partners += [xdev(d) for d in range(1, nx)] + [ydev(d) for d in range(1, ny)]
+    partners = [zdev(ahead(off)) for off in FAR] + [ydev(d) for d in sorted(
+        range(1, ny), key=lambda d: -min(d, ny - d))]
+    partners += [xdev(d) for d in range(1, nx)] + [sib]
     for dev in partners:
         pl.semaphore_signal(barrier, inc=1, device_id=dev, device_id_type=pl.DeviceIdType.MESH)
 
@@ -141,11 +141,11 @@
         for d in range(1, ny):
             send(pj_ref.at[:, mine], pj.at[c, y, x], PY, ydev(d))
         for off in FAR:
+            send(tblme, tblv.at[z], TBL, zdev(ahead(off)))
+        for off in FAR:
             zt = ahead(off)
             send(kvp.at[zt], kv.at[pl.ds(2 * s, 2)], KV, zdev(zt), KV + off)
         send(kvp.at[z], kv.at[pl.ds(2 * s, 2)], KVF, sib)
-        for off in FAR:
-            send(tblme, tblv.at[z], TBL, zdev(ahead(off)))
         for off in FAR:
             zt = ahead(off)
             send(qp.at[zt], qr.at[z], QS, zdev(zt))
@@ -157,6 +157,10 @@
         for d in range(1, nx):
             send(pj.at[c, :, x], pj.at[c, :, x], PX, xdev(d))
 
+    with jax.named_scope("tables"):
+        got(tblv.at[pl.ds(0, CHIPS - 1)], TBL)
+        table = pltpu.make_async_copy(tblv, tbls, lsem.at[0])
+        table.start()
     def forward(off):
         zf = behind(off)
         part = kv.at[pl.ds(4 * zf + 2 * c, 2)]
@@ -164,22 +168,14 @@
         send(part, part, KVF, sib)
         fill(2 * zf + c)
 
-    with jax.named_scope("forward_a"):
-        for off in NEAR[:4]:
+    with jax.named_scope("forward"):
+        for off in FAR:
             forward(off)
 
     with jax.named_scope("proj_rows_x"):
         got(pj.at[c, :, pl.ds(0, nx - 1)], PX)
         send(pj.at[c], pj.at[c], PS, sib)
 
-    with jax.named_scope("forward_b"):
-        for off in NEAR[4:]:
-            forward(off)
-
-    with jax.named_scope("tables"):
-        got(tblv.at[pl.ds(0, CHIPS - 1)], TBL)
-        table = pltpu.make_async_copy(tblv, tbls, lsem.at[0])
-        table.start()
     with jax.named_scope("proj_other"):
         got(pj.at[other], PS)
         loads[5].wait()
@@ -220,8 +216,8 @@
     def named(zs):
         return [list(fixed) + ids for _, fixed, ids in (slots(zs, b) for b in range(2))]
 
-    def softmax(zs):
-        biases = []
+    def biases(zs):
+        both = []
         for b in range(2):
             i, fixed, ids = slots(zs, b)
             valid = [i >= 1, i >= 0, i < BLOCKS - 1, i >= 2, i >= 3]
@@ -231,70 +227,62 @@
                 for earlier in ids[:n]:
                     clash = clash | (r == earlier)
                 valid.append(jnp.logical_not(clash))
-            biases.append([jnp.where(v, 0.0, NEG) for v in valid])
-        qf = qr[zs]
-        blocks = named(zs)
-        scores = dot(paired(kk, blocks), diagonal(qf, qf), ((1,), (1,)))
-        scores = jnp.concatenate([
-            scores[n * BLOCK:(n + 1) * BLOCK] + jnp.where(low[:1], biases[0][n], biases[1][n])
-            for n in range(8)], axis=0)
+            both.append([jnp.where(v, 0.0, NEG) for v in valid])
+        return both
+
+    def block(a, n):
+        return a[n * BLOCK:(n + 1) * BLOCK]
+
+    def fold(out):
+        return jnp.where(low, block(out, 0), block(out, 1)).astype(jnp.bfloat16)
+
+    def scored(zs):
+        bias = biases(zs)
+        scores = dot(paired(kk, named(zs)), diagonal(qr[zs], qr[zs]), ((1,), (1,)))
+        sst[zs] = jnp.concatenate([
+            block(scores, n) + jnp.where(low[:1], bias[0][n], bias[1][n]) for n in range(8)], axis=0)
+
+    def softmax(zs):
+        scores = sst[zs]
         top = jnp.max(scores, axis=0, keepdims=True)
         e = jnp.exp2((scores - top) * EXP2)
-        prob = (e * (1.0 / jnp.sum(e, axis=0, keepdims=True))).astype(jnp.bfloat16)
-        pst[zs] = prob
-        out = dot(prob, paired(vv, blocks), ((0,), (0,)))
-        ats[zs] = jnp.where(low, out[:BLOCK], out[BLOCK:]).astype(jnp.bfloat16)
-
-    def backward(zs):
+        pst[zs] = (e * (1.0 / jnp.sum(e, axis=0, keepdims=True))).astype(jnp.bfloat16)
+
+    def attended(zs):
+        ats[zs] = fold(dot(pst[zs], paired(vv, named(zs)), ((0,), (0,))))
+
+    def score_grads(zs):
+        gf = gr[zs]
+        dprob = dot(paired(vv, named(zs)), diagonal(gf, gf) * SCALE, ((1,), (1,)))
+        prob = pst[zs].astype(jnp.float32)
+        delta = jnp.sum(prob * dprob, axis=0, keepdims=True)
+        dst[zs] = (prob * (dprob - delta)).astype(jnp.bfloat16)
+
+    def query_grads(zs):
+        dqs[zs] = fold(dot(dst[zs], paired(kk, named(zs)), ((0,), (0,))))
+
+    def block_terms(zs):
         qf, gf = qr[zs], gr[zs]
+        prob, dscore = pst[zs], dst[zs]
+        left = jnp.concatenate([low] * 8, axis=0)
+        first = dot(jnp.where(left, dscore, swap(prob)), diagonal(qf, swap(gf)), ((1,), (0,)))
+        second = dot(jnp.where(left, swap(dscore), prob), diagonal(swap(qf), gf), ((1,), (0,)))
+        return first, second
+
+    def collect(zs, first, second):
         blocks = named(zs)
-        dprob = dot(paired(vv, blocks), diagonal(gf, gf) * SCALE, ((1,), (1,)))
-        low_prob = pst[zs]
-        prob = low_prob.astype(jnp.float32)
-        delta = jnp.sum(prob * dprob, axis=0, keepdims=True)
-        dscore = (prob * (dprob - delta)).astype(jnp.bfloat16)
-        out = dot(dscore, paired(kk, blocks), ((0,), (0,)))
-        dqs[zs] = jnp.where(low, out[:BLOCK], out[BLOCK:]).astype(jnp.bfloat16)
-        wide_low = jnp.concatenate([low] * 8, axis=0)
-        sides = (jnp.where(wide_low, dscore, swap(low_prob)),
-                 jnp.where(wide_low, swap(dscore), low_prob))
-        right = (diagonal(qf, swap(gf)), diagonal(swap(qf), gf))
-        terms = [dot(sides[b], right[b], ((1,), (0,))) for b in range(2)]
-        return blocks, terms
-
-    def collect(zs, blocks, terms):
-        for b in range(2):
-            for n in range(5):
-                acc[blocks[b][n]] += terms[b][n * BLOCK:(n + 1) * BLOCK]
+        acc[blocks[0][0]] += block(first, 0)
+        acc[blocks[0][1]] += block(first, 1) + block(second, 0)
+        acc[blocks[1][1]] += block(first, 2) + block(second, 1)
+        acc[blocks[1][2]] += block(second, 2)
+        for n in range(2):
+            acc[n] += block(first, 3 + n) + block(second, 3 + n)
+        for b, terms in enumerate((first, second)):
             for n in range(RANDOM):
-                trand[zs * 2 * RANDOM + RANDOM * b + n] = terms[b][(5 + n) * BLOCK:(6 + n) * BLOCK]
-
-    def far(step, n):
-        k = step * (PER // 2) + n // 2
-        return ahead(CHIPS // 2 - k if n % 2 else (CHIPS // 2 + 1 + k) % CHIPS)
+                trand[zs * 2 * RANDOM + RANDOM * b + n] = block(terms, 5 + n)
 
     def wide(ref):
         return ref.astype(jnp.float32)
-
-    with jax.named_scope("queries_wait"):
-        got(qr.at[pl.ds(0, CHIPS - 1)], QS)
-    with jax.named_scope("softmax"):
-        @pl.loop(0, CHIPS // PER)
-        def _(step):
-            sources = [far(step, n) for n in range(PER)]
-            for zs in sources:
-                softmax(zs)
-            for n, zs in enumerate(sources):
-                if n < PER - 2:
-                    send(ats.at[zs], atr.at[z], AT, zdev(zs))
-                elif n == PER - 1:
-                    send(ats.at[zs], atr.at[z], AT, zdev(zs))
-                else:
-                    @pl.when(step < CHIPS // PER - 1)
-                    def _():
-                        send(ats.at[zs], atr.at[z], AT, zdev(zs))
-
-        atr[z] = ats[z]
 
     def partial_proj():
         with jax.named_scope("attn_back"):
@@ -303,74 +291,80 @@
             attn = jnp.concatenate([
                 jnp.concatenate([atr[h][:, :HEAD_DIM] for h in range(HEADS)], axis=1),
                 jnp.concatenate([atr[h][:, HEAD_DIM:] for h in range(HEADS)], axis=1)], axis=0)
+            pp[1] = dot(attn, go_ref[0, :, theirs], ((0,), (0,))).astype(jnp.bfloat16)
+            send(pp.at[1], pps, RS, sib)
+            pp[0] = dot(attn, go_ref[0, :, mine], ((0,), (0,))).astype(jnp.bfloat16)
+
+    def proj_xy():
+        with jax.named_scope("grad_proj_core"):
+            got(pps, RS)
+            total = wide(pp[0]) + wide(pps[...])
+            s1[...] = total.astype(jnp.bfloat16).reshape(ny * nx, 16, HALF)
+            rx[dp] = s1[dp]
+            for dy in sorted(range(ny), key=lambda d: -min(d, ny - d)):
+                for dx in sorted(range(nx), key=lambda d: -min(d, nx - d)):
+                    if dx or dy:
+                        target = ((y + dy) % ny) * nx + (x + dx) % nx
+                        send(s1.at[target], rx.at[dp], RX, (target, s))
+
+    def proj_z():
+        with jax.named_scope("grad_proj_xy"):
+            got(rx.at[pl.ds(0, ny * nx - 1)], RX)
+            total = wide(rx[0])
+            for d in range(1, ny * nx):
+                total += wide(rx[d])
+            s3[...] = total.astype(jnp.bfloat16)
+            rz[s] = s3[...]
+            for off in FAR:
+                send(s3, rz.at[s], RZ, zdev(ahead(off)))
+                send(s3, rz.at[s], RZ, (dp, 2 * ahead(off) + other))
+            send(s3, rz.at[s], RZ, sib)
+
+    def proj_end():
+        with jax.named_scope("grad_proj_z"):
+            got(rz.at[pl.ds(0, 2 * CHIPS - 1)], RZ)
             for half in range(2):
-                f = slice(half * HALF, (half + 1) * HALF)
-                pp[half] = dot(attn, go_ref[0, :, f], ((0,), (0,))).astype(jnp.bfloat16)
-            send(pp.at[other], pps, RS, sib)
-
-    def proj_x():
-        with jax.named_scope("grad_proj_x"):
-            got(pps, RS)
-            total = wide(pp[c]) + wide(pps[...])
-            s1[...] = total.astype(jnp.bfloat16).reshape(ny, nx, 16, HALF)
-            for d in range(1, nx):
-                xt = (x + d) % nx
-                send(s1.at[:, xt], rx.at[d], RX, xdev(d))
-
-    def proj_y():
-        with jax.named_scope("grad_proj_y"):
-            total = wide(s1[:, x])
-            got(rx.at[pl.ds(1, nx - 1)], RX)
-            for d in range(1, nx):
-                total += wide(rx[d])
-            s2[...] = total.astype(jnp.bfloat16)
-            for d in range(1, ny):
-                send(s2.at[(y + d) % ny], ry.at[d], RY, ydev(d))
-
-    def proj_z():
-        with jax.named_scope("grad_proj_z"):
-            total = wide(s2[y])
-            got(ry.at[pl.ds(1, ny - 1)], RY)
-            for d in range(1, ny):
-                total += wide(ry[d])
-            s3[...] = total.astype(jnp.bfloat16)
-            rz[z] = s3[...]
-            for off in FAR:
-                send(s3, rz.at[z], RZ, zdev(ahead(off)))
-
-    def proj_core():
-        with jax.named_scope("grad_proj_core"):
-            got(rz.at[pl.ds(0, CHIPS - 1)], RZ)
-            total = wide(rz[0])
-            for k in range(1, CHIPS):
-                total += wide(rz[k])
-            s4[...] = total
-            send(s4, s4b, RF, sib)
-            gp_ref[:, mine] = total
+                total = wide(rz[half])
+                for k in range(1, CHIPS):
+                    total += wide(rz[2 * k + half])
+                gp_ref[:, half * HALF:(half + 1) * HALF] = total
+
+    with jax.named_scope("queries_wait"):
+        got(qr.at[pl.ds(0, CHIPS - 1)], QS)
+    with jax.named_scope("scores"):
+        for zs in range(CHIPS):
+            scored(zs)
+
+    with jax.named_scope("softmax"):
+        @pl.loop(0, CHIPS // PART)
+        def _(step):
+            for n in range(PART):
+                softmax(step * PART + n)
+    with jax.named_scope("attend"):
+        for zs in range(CHIPS):
+            attended(zs)
+        atr[z] = ats[z]
+        for off in FAR:
+            send(ats.at[ahead(off)], atr.at[z], AT, zdev(ahead(off)))
 
     with jax.named_scope("grad_attn_wait"):
         got(gr.at[pl.ds(0, CHIPS - 1)], GS)
-    with jax.named_scope("gradients"):
-        @pl.loop(0, CHIPS // PER)
+    with jax.named_scope("score_grads"):
+        for zs in range(CHIPS):
+            score_grads(zs)
+    with jax.named_scope("query_grads"):
+        for zs in range(CHIPS):
+            query_grads(zs)
+        dqr[z] = dqs[z]
+        for off in FAR:
+            send(dqs.at[ahead(off)], dqr.at[z], DQ, zdev(ahead(off)))
+    with jax.named_scope("block_terms"):
+        @pl.loop(0, CHIPS // PART)
         def _(step):
-            sources = [far(step, n) for n in range(PER)]
-            results = [backward(zs) for zs in sources]
-            for zs, (blocks, terms) in zip(sources, results):
-                collect(zs, blocks, terms)
-            for n, zs in enumerate(sources):
-                if n < PER - 2:
-                    send(dqs.at[zs], dqr.at[z], DQ, zdev(zs))
-                elif n == PER - 1:
-                    send(dqs.at[zs], dqr.at[z], DQ, zdev(zs))
-                else:
-                    @pl.when(step < CHIPS // PER - 1)
-                    def _():
-                        send(dqs.at[zs], dqr.at[z], DQ, zdev(zs))
-
+            results = [block_terms(step * PART + n) for n in range(PART)]
+            for n in range(PART):
+                collect(step * PART + n, *results[n])
             pl.when(step == 0)(partial_proj)
-            pl.when(step == 1)(proj_x)
-
-        dqr[z] = dqs[z]
 
     def pull(o):
         parts = [acc[2 * o], acc[2 * o + 1]]
@@ -390,6 +384,8 @@
                 xs[k, w] = parts[w].astype(jnp.bfloat16)
             send(xs.at[k], xr.at[k], XK, sib, XKR + off)
 
+    proj_xy()
+
     with jax.named_scope("own_terms"):
         @pl.loop(0, CHIPS)
         def _(step):
@@ -406,15 +402,12 @@
 
         dkr[z] = dks[z]
 
-    proj_y()
     proj_z()
 
     with jax.named_scope("grad_queries"):
         got(dqr.at[pl.ds(0, CHIPS - 1)], DQ)
         gq_ref[0, :BLOCK] = jnp.concatenate([dqr[h][:, :HEAD_DIM] for h in range(HEADS)], axis=1)
         gq_ref[0, BLOCK:] = jnp.concatenate([dqr[h][:, HEAD_DIM:] for h in range(HEADS)], axis=1)
-
-    proj_core()
 
     with jax.named_scope("grad_keys_values"):
         got(dkr.at[pl.ds(0, CHIPS - 1)], DK)
@@ -422,9 +415,7 @@
         gk_ref[0] = jnp.concatenate([p[:, :HEAD_DIM] for p in pieces], axis=1)
         gv_ref[0] = jnp.concatenate([p[:, HEAD_DIM:] for p in pieces], axis=1)
 
-    with jax.named_scope("grad_proj_end"):
-        got(s4b, RF)
-        gp_ref[:, theirs] = s4b[...]
+    proj_end()
 
     with jax.named_scope("sent"):
         rest = pl.ds(0, CHIPS - 1)
@@ -441,10 +432,8 @@
         sent(xs, XK)
         sent(dks.at[rest], DK)
         sent(pps, RS)
-        sent(s1.at[:, pl.ds(0, nx - 1)], RX)
-        sent(s2.at[pl.ds(0, ny - 1)], RY)
-        sent(rz.at[rest], RZ)
-        sent(s4, RF)
+        sent(rx.at[pl.ds(0, ny * nx - 1)], RX)
+        sent(rz.at[pl.ds(0, 2 * CHIPS - 1)], RZ)
 
 
 def store(*refs):
@@ -480,6 +469,8 @@
         pltpu.VMEM((HEADS, BLOCK, 128), bf),
         pltpu.VMEM((CHIPS, BLOCK, 128), bf),
         pltpu.VMEM((2, ny, nx, 16, HALF), bf),
+        pltpu.VMEM((CHIPS, 8 * BLOCK, 128), f32),
+        pltpu.VMEM((CHIPS, 8 * BLOCK, 128), bf),
         pltpu.VMEM((CHIPS, 8 * BLOCK, 128), bf),
         pltpu.VMEM((BLOCKS, BLOCK, 128), f32),
         pltpu.VMEM((CHIPS * 2 * RANDOM, BLOCK, 128), f32),
@@ -493,14 +484,10 @@
         pltpu.VMEM((HEADS, 2, BLOCK, 128), bf),
         pltpu.VMEM((2, rows, HALF), bf),
         pltpu.VMEM((rows, HALF), bf),
-        pltpu.VMEM((ny, nx, 16, HALF), bf),
-        pltpu.VMEM((nx, ny, 16, HALF), bf),
-        pltpu.VMEM((ny, 16, HALF), bf),
-        pltpu.VMEM((ny, 16, HALF), bf),
+        pltpu.VMEM((ny * nx, 16, HALF), bf),
+        pltpu.VMEM((ny * nx, 16, HALF), bf),
         pltpu.VMEM((16, HALF), bf),
-        pltpu.VMEM((CHIPS, 16, HALF), bf),
-        pltpu.VMEM((16, HALF), f32),
-        pltpu.VMEM((16, HALF), f32),
+        pltpu.VMEM((2 * CHIPS, 16, HALF), bf),
         pltpu.SemaphoreType.DMA((SEMS,)),
         pltpu.SemaphoreType.DMA((SEMS,)),
         pltpu.SemaphoreType.DMA((7,)),

time: 55.2 us -> 52.5 us (0.951)
  Pallas kernels: 54.4 us -> 51.7 us
    pallas_call x1, Pallas kernels: 53.6 us -> 50.9 us  [attention_grads(): pl.pallas_call(functools.partial(kernel, nx, ny), out_shape=shapes, in_sp...]
where the time goes in v4:
time: 52.5 us; the launch traced here: 52.4 us
  Pallas kernels  51.7 us (98%)
  between operations  0.64 us (1%)
    pallas_call x1, Pallas kernels, attention_grads(): pl.pallas_call(functools.partial(kernel, nx, ny), out_shape=shapes, in_sp...  50.9 us

profile of v4, /device:TPU:1, one launch (start us, length us, event | category | flops | bytes accessed | tf_op | source)
XLA Modules:
  0.0 52.4 jit_solution(6557723529623458647)
XLA Ops:
  0.6 50.9 %shard_map.93 = (bf16[1,128,512]{2,1,0:T(8,128)(2,1)S(1)}, bf16[1,128,512]{2,1,0:T(8,128)(2,1)S(1)}, bf16[1,128,512]{2,1,0:T(8,128)(2,1)S(1)}, f32[16,512]{1,0:T(8,128)S(1)}) custom-call(bf16[1,128,512]{2,1,0:T(8,128)(2,1)} %q_hbm.1, bf16[1,128,512]{2,1,0:T(8,128)(2,1)} %k_hbm.1, bf16[1,128,512]{2,1,0:T(8,128)(2,1)} %v_hbm.1, bf16[1,128,512]{2,1,0:T(8,128)(2,1)} %go_hbm.1, ...), custom_call_target="tpu_custom_call" | custom-call | flops 1000000000 | bytes 2000000 | tf_op jit(solution)/shard_map/pallas_call | solution.py:497
  51.6 0.8 %shard_map.94 = (bf16[1,128,512]{2,1,0:T(8,128)(2,1)}, bf16[1,128,512]{2,1,0:T(8,128)(2,1)}, bf16[1,128,512]{2,1,0:T(8,128)(2,1)}, f32[16,512]{1,0:T(8,128)}) custom-call(bf16[1,128,512]{2,1,0:T(8,128)(2,1)S(1)} %get-tuple-element.8.refs_0_, bf16[1,128,512]{2,1,0:T(8,128)(2,1)S(1)} %get-tuple-element.9.refs_1_, ...), custom_call_target="tpu_custom_call" | custom-call | tf_op jit(solution)/shard_map/pallas_call | solution.py:508

commit v5 on v4

--- a/solution.py
+++ b/solution.py
@@ -22,8 +22,9 @@
 PART = 4
 VMEM = 40 * 1024 * 1024
 
-KVF, QS, GS, TBL, PY, PX, PS, AT, DQ, XK, DK, RS, RX, RZ = range(14)
-KV, XKR, SEMS = 16, 24, 32
+KVF, QS, GS, TBL, PY, PX, PS, AT, DQ, XK, DK, RS, RX, RZ, KVS = range(15)
+SENDS = 15
+KV, XKR, RECVS = 16, 24, 32
 EXP2 = SCALE * 1.4426950408889634
 
 
@@ -79,9 +80,10 @@
         return (z + CHIPS - off) % CHIPS
 
     barrier = pltpu.get_barrier_semaphore()
-    partners = [zdev(ahead(off)) for off in FAR] + [ydev(d) for d in sorted(
-        range(1, ny), key=lambda d: -min(d, ny - d))]
-    partners += [xdev(d) for d in range(1, nx)] + [sib]
+    hops = [(min(off, CHIPS - off), zdev(ahead(off))) for off in range(1, CHIPS)]
+    hops += [(min(d, ny - d), ydev(d)) for d in range(1, ny)]
+    hops += [(min(d, nx - d), xdev(d)) for d in range(1, nx)] + [(0, sib)]
+    partners = [dev for _, dev in sorted(hops, key=lambda item: -item[0])]
     for dev in partners:
         pl.semaphore_signal(barrier, inc=1, device_id=dev, device_id_type=pl.DeviceIdType.MESH)
 
@@ -144,7 +146,7 @@
             send(tblme, tblv.at[z], TBL, zdev(ahead(off)))
         for off in FAR:
             zt = ahead(off)
-            send(kvp.at[zt], kv.at[pl.ds(2 * s, 2)], KV, zdev(zt), KV + off)
+            send(kvp.at[zt], kv.at[pl.ds(2 * s, 2)], KVS, zdev(zt), KV + off)
         send(kvp.at[z], kv.at[pl.ds(2 * s, 2)], KVF, sib)
         for off in FAR:
             zt = ahead(off)
@@ -301,8 +303,8 @@
             total = wide(pp[0]) + wide(pps[...])
             s1[...] = total.astype(jnp.bfloat16).reshape(ny * nx, 16, HALF)
             rx[dp] = s1[dp]
-            for dy in sorted(range(ny), key=lambda d: -min(d, ny - d)):
-                for dx in sorted(range(nx), key=lambda d: -min(d, nx - d)):
+            for dx in sorted(range(nx), key=lambda d: -min(d, nx - d)):
+                for dy in sorted(range(ny), key=lambda d: -min(d, ny - d)):
                     if dx or dy:
                         target = ((y + dy) % ny) * nx + (x + dx) % nx
                         send(s1.at[target], rx.at[dp], RX, (target, s))
@@ -331,18 +333,14 @@
 
     with jax.named_scope("queries_wait"):
         got(qr.at[pl.ds(0, CHIPS - 1)], QS)
-    with jax.named_scope("scores"):
-        for zs in range(CHIPS):
-            scored(zs)
-
-    with jax.named_scope("softmax"):
-        @pl.loop(0, CHIPS // PART)
-        def _(step):
-            for n in range(PART):
-                softmax(step * PART + n)
-    with jax.named_scope("attend"):
-        for zs in range(CHIPS):
-            attended(zs)
+    with jax.named_scope("attention"):
+        for n in range(CHIPS + 2 * PART):
+            if n < CHIPS:
+                scored(n)
+            if PART <= n < CHIPS + PART:
+                softmax(n - PART)
+            if 2 * PART <= n:
+                attended(n - 2 * PART)
         atr[z] = ats[z]
         for off in FAR:
             send(ats.at[ahead(off)], atr.at[z], AT, zdev(ahead(off)))
@@ -423,7 +421,7 @@
         sent(pj.at[0, :, pl.ds(0, nx - 1)], PX)
         sent(pj.at[0], PS)
         sent(tblv.at[rest], TBL)
-        sent(kvp.at[rest], KV)
+        sent(kvp.at[rest], KVS)
         sent(kvp, KVF)
         sent(qp.at[rest], QS)
         sent(gpk.at[rest], GS)
@@ -488,8 +486,8 @@
         pltpu.VMEM((ny * nx, 16, HALF), bf),
         pltpu.VMEM((16, HALF), bf),
         pltpu.VMEM((2 * CHIPS, 16, HALF), bf),
-        pltpu.SemaphoreType.DMA((SEMS,)),
-        pltpu.SemaphoreType.DMA((SEMS,)),
+        pltpu.SemaphoreType.DMA((SENDS,)),
+        pltpu.SemaphoreType.DMA((RECVS,)),
         pltpu.SemaphoreType.DMA((7,)),
     ]
     tokens = jax.ShapeDtypeStruct((1, TOKENS, WIDTH), bf)

time: 52.5 us -> 52.1 us (level)
  no operation moved by 1% of the time
where the time goes in v5:
time: 52.1 us; the launch traced here: 51.9 us
  Pallas kernels  51.3 us (98%)
  between operations  0.64 us (1%)
    pallas_call x1, Pallas kernels, attention_grads(): pl.pallas_call(functools.partial(kernel, nx, ny), out_shape=shapes, in_sp...  50.5 us

profile of v5, /device:TPU:1, one launch (start us, length us, event | category | flops | bytes accessed | tf_op | source)
XLA Modules:
  0.0 51.9 jit_solution(7442458678947945487)
XLA Ops:
  0.6 50.5 %shard_map.93 = (bf16[1,128,512]{2,1,0:T(8,128)(2,1)S(1)}, bf16[1,128,512]{2,1,0:T(8,128)(2,1)S(1)}, bf16[1,128,512]{2,1,0:T(8,128)(2,1)S(1)}, f32[16,512]{1,0:T(8,128)S(1)}) custom-call(bf16[1,128,512]{2,1,0:T(8,128)(2,1)} %q_hbm.1, bf16[1,128,512]{2,1,0:T(8,128)(2,1)} %k_hbm.1, bf16[1,128,512]{2,1,0:T(8,128)(2,1)} %v_hbm.1, bf16[1,128,512]{2,1,0:T(8,128)(2,1)} %go_hbm.1, ...), custom_call_target="tpu_custom_call" | custom-call | flops 1000000000 | bytes 2000000 | tf_op jit(solution)/shard_map/pallas_call | solution.py:495
  51.1 0.8 %shard_map.94 = (bf16[1,128,512]{2,1,0:T(8,128)(2,1)}, bf16[1,128,512]{2,1,0:T(8,128)(2,1)}, bf16[1,128,512]{2,1,0:T(8,128)(2,1)}, f32[16,512]{1,0:T(8,128)}) custom-call(bf16[1,128,512]{2,1,0:T(8,128)(2,1)S(1)} %get-tuple-element.8.refs_0_, bf16[1,128,512]{2,1,0:T(8,128)(2,1)S(1)} %get-tuple-element.9.refs_1_, ...), custom_call_target="tpu_custom_call" | custom-call | tf_op jit(solution)/shard_map/pallas_call | solution.py:506

commit v6 on v5

--- a/solution.py
+++ b/solution.py
@@ -293,8 +293,11 @@
             attn = jnp.concatenate([
                 jnp.concatenate([atr[h][:, :HEAD_DIM] for h in range(HEADS)], axis=1),
                 jnp.concatenate([atr[h][:, HEAD_DIM:] for h in range(HEADS)], axis=1)], axis=0)
-            pp[1] = dot(attn, go_ref[0, :, theirs], ((0,), (0,))).astype(jnp.bfloat16)
-            send(pp.at[1], pps, RS, sib)
+            for first in range(0, WIDTH, HALF):
+                upper = attn[:, first:first + HALF]
+                part = pl.ds(first, HALF)
+                pp[1, part] = dot(upper, go_ref[0, :, theirs], ((0,), (0,))).astype(jnp.bfloat16)
+                send(pp.at[1, part], pps.at[part], RS, sib)
             pp[0] = dot(attn, go_ref[0, :, mine], ((0,), (0,))).astype(jnp.bfloat16)
 
     def proj_xy():

time: 52.1 us -> 52.2 us (level)
  no operation moved by 1% of the time
where the time goes in v6:
time: 52.2 us; the launch traced here: 52.1 us
  Pallas kernels  51.4 us (98%)
  between operations  0.64 us (1%)
    pallas_call x1, Pallas kernels, attention_grads(): pl.pallas_call(functools.partial(kernel, nx, ny), out_shape=shapes, in_sp...  50.7 us

profile of v6, /device:TPU:1, one launch (start us, length us, event | category | flops | bytes accessed | tf_op | source)
XLA Modules:
  0.0 52.1 jit_solution(10161169902393300130)
XLA Ops:
  0.6 50.7 %shard_map.93 = (bf16[1,128,512]{2,1,0:T(8,128)(2,1)S(1)}, bf16[1,128,512]{2,1,0:T(8,128)(2,1)S(1)}, bf16[1,128,512]{2,1,0:T(8,128)(2,1)S(1)}, f32[16,512]{1,0:T(8,128)S(1)}) custom-call(bf16[1,128,512]{2,1,0:T(8,128)(2,1)} %q_hbm.1, bf16[1,128,512]{2,1,0:T(8,128)(2,1)} %k_hbm.1, bf16[1,128,512]{2,1,0:T(8,128)(2,1)} %v_hbm.1, bf16[1,128,512]{2,1,0:T(8,128)(2,1)} %go_hbm.1, ...), custom_call_target="tpu_custom_call" | custom-call | flops 1000000000 | bytes 2000000 | tf_op jit(solution)/shard_map/pallas_call | solution.py:498
  51.3 0.8 %shard_map.94 = (bf16[1,128,512]{2,1,0:T(8,128)(2,1)}, bf16[1,128,512]{2,1,0:T(8,128)(2,1)}, bf16[1,128,512]{2,1,0:T(8,128)(2,1)}, f32[16,512]{1,0:T(8,128)}) custom-call(bf16[1,128,512]{2,1,0:T(8,128)(2,1)S(1)} %get-tuple-element.8.refs_0_, bf16[1,128,512]{2,1,0:T(8,128)(2,1)S(1)} %get-tuple-element.9.refs_1_, ...), custom_call_target="tpu_custom_call" | custom-call | tf_op jit(solution)/shard_map/pallas_call | solution.py:509
